TPU v7x, 256 devices: a whole 4x4x8 slice. The times are simulated.
256 devices in a mesh: trow: 32 (over z, x), mode: 8 (over y, core).
Axes of the slice: x: 4, y: 4, z: 8, core: 2. Of those that a mesh axis runs over, the one named last changes fastest.
Arguments:
- g_hist: bfloat16 [2, 64, 64, 128, 128], P(None, 'trow', None, 'mode'), may hold values from -4 to 4
- new_cols: bfloat16 [2, 64, 8, 128, 128], P(None, 'trow', None, 'mode'), may hold values from -4 to 4
- row_time: int32 [64], replicated, may hold values from 0 to 63, as said below
- drive_step: int32 [64], replicated, may hold values from 0 to 15
- drive_levels: float32 [16, 128], replicated, may hold values from 0.5 to 1.5
Outputs:
- collision: float32 [2, 64, 8, 128, 128], P(None, 'trow', None, 'mode')
Inputs may be any that keep to these rules, and one draw needn't show every extreme that they name: `row_time`: the 2 row slots of one index of trow hold 2 consecutive times in rising order, the first a multiple of 2; every time is held by exactly one slot.
All inputs are finite; a program needn't handle non-finite values.
Results may differ from a plain program's by a relative error of at most 0.0029.
Values may be sent and summed in bfloat16 or wider, within the bound.
A program may use at most 128 MiB of HBM per device.

v0:
```python
import jax
import jax.numpy as jnp
from jax import lax
from jax.sharding import PartitionSpec as P

TIME_SPAN = 8.0


def body(g_hist, new_cols, row_time, drive_step, drive_levels):
    rows_here = g_hist.shape[1]
    slot_count = g_hist.shape[2]
    shard_width = g_hist.shape[3]
    mode_count = g_hist.shape[4]
    level_count = drive_levels.shape[0]
    trow_size = lax.axis_size("trow")
    trow_rank = lax.axis_index("trow")
    mode_rank = lax.axis_index("mode")
    time_grid = jnp.arange(slot_count, dtype=jnp.int32)
    match_time = row_time[:, None] == time_grid[None, :]
    slot_level = jnp.sum(jnp.where(match_time, drive_step[None, :], 0), axis=1)
    level_table = (slot_level[:, None] == jnp.arange(level_count, dtype=jnp.int32)[None, :]).astype(
        jnp.float32
    )
    kerr_slot = jnp.dot(level_table, drive_levels, precision=lax.Precision.HIGHEST)
    kerr_own = lax.dynamic_slice_in_dim(kerr_slot, trow_rank * rows_here, rows_here, 0)
    kerr_mine = lax.dynamic_slice_in_dim(kerr_slot, mode_rank * shard_width, shard_width, 1)
    own_times = lax.dynamic_slice_in_dim(row_time, trow_rank * rows_here, rows_here, 0)
    reordered = jnp.take(g_hist, row_time, axis=2)
    outgoing = reordered.reshape(2, rows_here, trow_size, rows_here, shard_width, mode_count)
    outgoing = jnp.transpose(outgoing, (0, 2, 1, 3, 5, 4))
    incoming = lax.all_to_all(
        lax.all_to_all(outgoing, "trow", split_axis=1, concat_axis=1, tiled=True),
        "mode",
        split_axis=4,
        concat_axis=5,
        tiled=True,
    )
    incoming = incoming.reshape(2, slot_count, rows_here, shard_width, mode_count)
    mirror = jnp.transpose(incoming, (0, 2, 1, 3, 4)).astype(jnp.float32)
    green = reordered.astype(jnp.float32)
    green_re = green[0]
    green_im = green[1]
    square_re = green_re * green_re - green_im * green_im
    square_im = 2.0 * green_re * green_im
    bubble_re = square_re * mirror[0] - square_im * mirror[1]
    bubble_im = square_re * mirror[1] + square_im * mirror[0]
    coupling = kerr_own[:, None, None, :] * kerr_mine[None, :, :, None]
    live = (row_time[None, :] <= own_times[:, None])[:, :, None, None]
    sigma_re = jnp.where(live, bubble_re * coupling, 0.0).astype(jnp.bfloat16)
    sigma_im = jnp.where(live, bubble_im * coupling, 0.0).astype(jnp.bfloat16)
    portion = lax.all_gather(new_cols, "trow", axis=1, tiled=True)
    column_re = portion[0]
    column_im = portion[1]
    total_re = jnp.einsum(
        "rkyx,knyb->rnxb", sigma_re, column_re, preferred_element_type=jnp.float32
    ) - jnp.einsum("rkyx,knyb->rnxb", sigma_im, column_im, preferred_element_type=jnp.float32)
    total_im = jnp.einsum(
        "rkyx,knyb->rnxb", sigma_re, column_im, preferred_element_type=jnp.float32
    ) + jnp.einsum("rkyx,knyb->rnxb", sigma_im, column_re, preferred_element_type=jnp.float32)
    total_re, total_im = (total_re, total_im)
    partials = jnp.stack([total_re, total_im])
    reduced = lax.psum_scatter(partials, "mode", scatter_dimension=3, tiled=True)
    return TIME_SPAN / slot_count * reduced


def solution(mesh):
    placed = (
        P(None, "trow", None, "mode", None),
        P(None, "trow", None, "mode", None),
        P(),
        P(),
        P(),
    )
    return jax.shard_map(
        body,
        mesh=mesh,
        in_specs=placed,
        out_specs=P(None, "trow", None, "mode", None),
        check_vma=False,
    )
```

profile of v0, /device:TPU:1, one launch (start us, length us, event | category | flops | bytes accessed | tf_op | source)
XLA Modules:
  0.0 175.9 jit_solution(18220939505481382031)
XLA Ops:
  6.5 0.0 copy-start
  6.5 0.0 all-gather.2.cloned.1.call-start
  6.5 1.7 copy.55
  8.2 0.0 all-gather.2.cloned.1.call-update
  8.2 0.7 compare_select_fusion
  8.9 0.0 copy-done
  8.9 0.0 copy-start.4
  8.9 0.8 gather_fusion
  9.7 0.2 copy.49
  9.9 0.0 copy-done.4
  9.9 0.1 broadcast_in_dim.60
  10.0 0.2 select_bitcast_fusion
  10.2 0.0 copy-start.6
  10.2 1.2 copy.50
  11.4 11.9 %all-to-all-start = ((bf16[2,32,2,2,128,16]{4,5,3,2,0,1:T(8,128)(2,1)}), bf16[2,32,2,2,128,16]{4,5,3,2,0,1:T(8,128)(2,1)S(1)}, u32[]{:S(2)}, u32[]{:S(2)}) async-start(bf16[2,32,2,2,128,16]{4,5,3,2,0,1:T(8,128)(2,1)} %copy.50), calls=%async_computation | async-start | bytes 2097152 | tf_op jit(solution)/shard_map/all_to_all | solution.py:32
  23.3 0.1 dynamic_slice.9
  23.4 0.0 copy-done.6
  23.4 0.2 select_reduce_fusion
  23.6 28.7 %all-to-all-done = bf16[2,32,2,2,128,16]{4,5,3,2,0,1:T(8,128)(2,1)S(1)} async-done(((bf16[2,32,2,2,128,16]{4,5,3,2,0,1:T(8,128)(2,1)}), bf16[2,32,2,2,128,16]{4,5,3,2,0,1:T(8,128)(2,1)S(1)}, u32[]{:S(2)}, u32[]{:S(2)}) %all-to-all-start) | async-done | bytes 1048608 | tf_op jit(solution)/shard_map/all_to_all | solution.py:32
  52.2 6.8 %copy.51 = bf16[2,32,2,2,128,16]{1,5,3,2,0,4:T(8,128)(2,1)} copy(bf16[2,32,2,2,128,16]{4,5,3,2,0,1:T(8,128)(2,1)S(1)} %all-to-all-done) | data formatting | bytes 2097152 | tf_op jit(solution)/shard_map/all_to_all | solution.py:32
  59.0 7.8 %reshape.75 = bf16[8,2,32768]{2,1,0:T(2,128)(2,1)} reshape(bf16[128,2,2,2,16,32]{5,4,3,2,1,0:T(8,128)(2,1)} %bitcast.81) | data formatting | bytes 2097152
  66.9 0.0 copy-start.5
  66.9 8.2 %all-to-all-start.1 = ((bf16[8,2,32768]{2,1,0:T(2,128)(2,1)}), bf16[8,2,32768]{2,1,0:T(2,128)(2,1)S(1)}, u32[]{:S(2)}, u32[]{:S(2)}) async-start(bf16[8,2,32768]{2,1,0:T(2,128)(2,1)} %reshape.75), calls=%async_computation.1 | async-start | bytes 2097152 | tf_op jit(solution)/shard_map/all_to_all | solution.py:31
  75.0 0.0 reduce-scatter.2.cloned.1.call-start
  75.0 0.0 copy-done.5
  75.1 0.2 fusion.22
  75.3 0.1 constant_dynamic-slice_fusion.1
  75.4 0.1 broadcast_compare_fusion
  75.4 1.5 select_convert_fusion
  77.0 13.2 %all-to-all-done.1 = bf16[8,2,32768]{2,1,0:T(2,128)(2,1)S(1)} async-done(((bf16[8,2,32768]{2,1,0:T(2,128)(2,1)}), bf16[8,2,32768]{2,1,0:T(2,128)(2,1)S(1)}, u32[]{:S(2)}, u32[]{:S(2)}) %all-to-all-start.1) | async-done | bytes 1048608 | tf_op jit(solution)/shard_map/all_to_all | solution.py:31
  90.1 4.5 %reshape.76 = bf16[128,2,2,2,16,32]{5,4,3,2,1,0:T(8,128)(2,1)} reshape(bf16[8,2,32768]{2,1,0:T(2,128)(2,1)S(1)} %all-to-all-done.1) | data formatting | bytes 2097152
  94.6 2.9 %copy.52 = bf16[2,32,2,2,128,16]{1,5,4,3,2,0:T(8,128)(2,1)S(1)} copy(bf16[2,32,2,2,128,16]{1,5,3,2,0,4:T(8,128)(2,1)} %bitcast.83) | data formatting | bytes 2097152 | tf_op jit(solution)/shard_map/all_to_all | solution.py:31
  97.6 4.4 %convert_bitcast_fusion = f32[2,32,2,2,16,8,16]{1,6,4,5,3,2,0:T(8,128)} fusion(bf16[2,32,2,2,8,16,16]{1,6,5,4,3,2,0:T(8,128)(2,1)S(1)} %bitcast.82), kind=kLoop, calls=%fused_computation.1 | loop fusion | flops 524288 | bytes 3145728 | tf_op jit(solution)/shard_map/convert_element_type | solution.py:39
  102.0 15.9 %copy.68 = f32[2,32,2,2,16,8,16]{6,5,4,3,0,2,1:T(8,128)} copy(f32[2,32,2,2,16,8,16]{1,6,4,5,3,2,0:T(8,128)} %convert_bitcast_fusion) | data formatting | bytes 4194304 | tf_op jit(solution)/shard_map/convert_element_type | solution.py:39
  117.9 10.3 %reshape.74 = f32[2,64,2,16,128]{4,3,2,0,1:T(8,128)S(1)} reshape(f32[2,32,2,2,16,8,16]{6,5,4,3,0,2,1:T(8,128)} %copy.68) | data formatting | bytes 4194304 | tf_op jit(solution)/shard_map/convert_element_type | solution.py:39
  128.2 2.8 %fusion.16 = (bf16[2,64,16,128,1]{3,2,0,1,4:T(8,128)(2,1)}, bf16[2,64,16,128,1]{3,2,0,1,4:T(8,128)(2,1)}) fusion(f32[2,2,64,16,128]{4,3,1,0,2:T(8,128)S(1)} %bitcast.85, f32[64,16]{1,0:T(8,128)S(1)} %constant_dynamic-slice_fusion.1, f32[2,128]{1,0:T(2,128)S(1)} %constant_dynamic-slice_fusion, pred[2,64]{0,1:T(8,128)(4,1)S(1)} %broadcast_compare_fusion, ...), kind=kLoop, calls=%fused_computation.27 | loop fusion | flops 4718592 | bytes 5248128 | tf_op jit(solution)/shard_map/convert_element_type | solution.py:50
  131.0 2.6 %fusion.4 = f32[2,128,8,128]{3,1,2,0:T(8,128)S(1)} fusion(bf16[2,64,8,16,128]{4,3,1,2,0:T(8,128)(2,1)} %all-gather.2.cloned.1.call-done, bf16[2,64,16,128,1]{3,2,0,1,4:T(8,128)(2,1)} %get-tuple-element.5), kind=kOutput, calls=%fused_computation.11 | convolution fusion | flops 536870912 | bytes 3670016 | tf_op jit(solution)/shard_map/rkyx,knyb->rnxb/dot_general | solution.py:56
  133.6 0.3 copy-done.1
  134.0 0.1 copy-done.3
  134.1 0.7 fusion.5
  134.8 0.0 copy-start.2
  134.8 0.7 fusion.11
  135.6 0.3 copy-done.2
  135.9 0.7 fusion.9
  136.6 1.6 pad_maximum_fusion
  138.2 0.0 reduce-scatter.2.cloned.1.call-update
  138.2 29.2 %reduce-scatter.2.cloned.1.call-done = f32[2,2,8,16,128]{4,3,2,1,0:T(8,128)} async-done(((f32[2,2,8,128,128]{4,3,2,1,0:T(8,128)}), f32[2,2,8,16,128]{4,3,2,1,0:T(8,128)}) %reduce-scatter.2.cloned.1.call-update) | async-done | bytes 262160 | tf_op jit(solution)/shard_map/reduce_scatter | solution.py:62
  167.4 1.7 broadcast_multiply_fusion
  (6 shorter events, 0.0 us)
Async XLA Ops:
  6.5 2.4 %copy-start = (bf16[2,2,64,16,128]{4,3,2,1,0:T(8,128)(2,1)S(1)}, bf16[2,2,64,16,128]{4,3,2,1,0:T(8,128)(2,1)}, u32[]{:S(2)}) copy-start(bf16[2,2,64,16,128]{4,3,2,1,0:T(8,128)(2,1)} %param.5) | copy-start | bytes 3145732
  6.5 124.5 %all-gather.2.cloned.1.call-start = ((), (), s32[]{:S(2)}) async-start(), calls=%async_computation.3 | async-start | bytes 4325376 | tf_op jit(solution)/shard_map/all_gather | solution.py:51
  8.9 1.0 copy-start.4
  10.2 13.2 %copy-start.6 = (s32[64]{0:T(128)S(1)}, s32[64]{0:T(128)}, u32[]{:S(2)}) copy-start(s32[64]{0:T(128)} %param.8) | copy-start | bytes 772
  11.4 40.8 %all-to-all-start = ((bf16[2,32,2,2,128,16]{4,5,3,2,0,1:T(8,128)(2,1)}), bf16[2,32,2,2,128,16]{4,5,3,2,0,1:T(8,128)(2,1)S(1)}, u32[]{:S(2)}, u32[]{:S(2)}) async-start(bf16[2,32,2,2,128,16]{4,5,3,2,0,1:T(8,128)(2,1)} %copy.50), calls=%async_computation | async-start | bytes 2097152 | tf_op jit(solution)/shard_map/all_to_all | solution.py:32
  66.9 8.2 %copy-start.5 = (f32[16,128]{1,0:T(8,128)S(1)}, f32[16,128]{1,0:T(8,128)}, u32[]{:S(2)}) copy-start(f32[16,128]{1,0:T(8,128)} %param.9) | copy-start | bytes 24580
  66.9 23.3 %all-to-all-start.1 = ((bf16[8,2,32768]{2,1,0:T(2,128)(2,1)}), bf16[8,2,32768]{2,1,0:T(2,128)(2,1)S(1)}, u32[]{:S(2)}, u32[]{:S(2)}) async-start(bf16[8,2,32768]{2,1,0:T(2,128)(2,1)} %reshape.75), calls=%async_computation.1 | async-start | bytes 2097152 | tf_op jit(solution)/shard_map/all_to_all | solution.py:31
  75.0 92.3 %reduce-scatter.2.cloned.1.call-start = ((), (), s32[]{:S(2)}) async-start(), calls=%async_computation.4 | async-start | bytes 2359296 | tf_op jit(solution)/shard_map/reduce_scatter | solution.py:62
  131.0 3.0 %copy-start.1 = (bf16[2,64,8,16,128]{4,3,1,2,0:T(8,128)(2,1)S(1)}, bf16[2,64,8,16,128]{4,3,1,2,0:T(8,128)(2,1)}, u32[]{:S(2)}) copy-start(bf16[2,64,8,16,128]{4,3,1,2,0:T(8,128)(2,1)} %all-gather.2.cloned.1.call-done) | copy-start | bytes 12582916
  131.0 3.1 %copy-start.3 = (bf16[2,64,16,128,1]{3,2,0,1,4:T(8,128)(2,1)S(1)}, bf16[2,64,16,128,1]{3,2,0,1,4:T(8,128)(2,1)}, u32[]{:S(2)}) copy-start(bf16[2,64,16,128,1]{3,2,0,1,4:T(8,128)(2,1)} %get-tuple-element.6) | copy-start | bytes 1572868
  134.8 1.0 copy-start.2
Sparse Core Ops, SparseCore 0:
  9.8 90.8 all-gather.1
  138.3 29.0 reduce-scatter.1
where the time goes:
time: 179 us; the launch traced here: 176 us
  waiting for transfers between devices  71 us (40%)
  local copies, waits for them, and re-layouts  53.2 us (30%)
  starting transfers between devices  20 us (11%)
  between operations  13.6 us (8%)
  other arithmetic  13 us (7%)
  matrix products  5 us (3%)
    reduce_scatter x1, waiting for transfers between devices, body(): lax.psum_scatter(partials, 'mode', scatter_dimension=3, tiled=True)  29.2 us
    all_to_all x1, waiting for transfers between devices, body(): lax.all_to_all(outgoing, 'trow', split_axis=1, concat_axis=1, tiled=True)  28.7 us
    convert_element_type x2, local copies, waits for them, and re-layouts, body(): mirror = jnp.transpose(incoming, (0, 2, 1, 3, 4)).astype(jnp.float32)  26.2 us
    unnamed x17, local copies, waits for them, and re-layouts  14.8 us
    all_to_all x1, waiting for transfers between devices, body(): lax.all_to_all(lax.all_to_all(outgoing, 'trow', split_axis=1, concat_axis...  13.2 us
    all_to_all x1, starting transfers between devices, body(): lax.all_to_all(outgoing, 'trow', split_axis=1, concat_axis=1, tiled=True)  11.9 us
    all_to_all x1, starting transfers between devices, body(): lax.all_to_all(lax.all_to_all(outgoing, 'trow', split_axis=1, concat_axis...  8.18 us
    all_to_all x1, local copies, waits for them, and re-layouts, body(): lax.all_to_all(outgoing, 'trow', split_axis=1, concat_axis=1, tiled=True)  6.83 us
  transfers between devices with their start and end apart: 4, of which 3 were waited for; matrix products, arithmetic and copies ran while one was open for 35% of the time, Pallas kernels for 0%

commit v1 on v0

v1 whole, which is shorter than its diff:
```python
import jax
import jax.numpy as jnp
from jax import lax
from jax.experimental import pallas as pl
from jax.experimental.pallas import tpu as pltpu
from jax.sharding import PartitionSpec as P

NZ, NX, NY, NCORE = 8, 4, 4, 2
NR, NMODE = NZ * NX, NY * NCORE
BF, F32 = jnp.bfloat16, jnp.float32
MESH = pl.DeviceIdType.MESH

DZ = (4, 3, 5, 2, 6, 1, 7, 0)
A1, A2 = (0, 384), (384, 384)
A = (0, 768)
B1, B2 = (768, 128), (896, 128)
B = (768, 256)
SCALE = 8.0 / 64


def kernel(
    rt, ds, dl, g, c, out,
    sb, rb, tb, mb, sq, lhs, rhs, part, cb, red, yb, kb,
    s1_send, s1_recv, s2_send, s2_recv,
    za_s, za_r, xa_s, xa_r, xb_s, xb_r, zb_s, zb_r,
    cx_s, cx_r, yx_s, yx_r,
):
    r = lax.axis_index("trow")
    m = lax.axis_index("mode")
    z, x = r // NX, r % NX
    y, core = m // NCORE, m % NCORE

    def at_z(d):
        return (z + d + NZ) % NZ

    def at_x(d):
        return (x + d + NX) % NX

    def trow_dev(zz, xx):
        return {"trow": zz * NX + xx, "mode": m}

    bar = pltpu.get_barrier_semaphore()

    def greet_trow(j, _):
        pl.semaphore_signal(bar, inc=1, device_id={"trow": (r + 1 + j) % NR, "mode": m}, device_id_type=MESH)
        return 0

    def greet_mode(j, _):
        pl.semaphore_signal(bar, inc=1, device_id={"trow": r, "mode": (m + 1 + j) % NMODE}, device_id_type=MESH)
        return 0

    lax.fori_loop(0, NR - 1, greet_trow, 0)
    lax.fori_loop(0, NMODE - 1, greet_mode, 0)

    for p in range(2):
        for k in range(2):
            for n in range(8):
                rhs[z, p, x, pl.ds(16 * k, 16), pl.ds(128 * n, 128)] = c[p, k, n]

    def fill(q, _):
        for i in range(2):
            t = rt[2 * q + i]
            for p in range(2):
                for o in range(2):
                    sb[q, p, i, o] = g[p, o, t]
        return 0

    lax.fori_loop(0, NR, fill, 0)
    rb[r] = sb[r]

    pl.semaphore_wait(bar, NR - 1 + NMODE - 1)

    sent = []

    def push(zz, xx, lanes, s, rsem, dev):
        ref = rhs.at[zz, :, xx, :, pl.ds(*lanes)] if xx is not None else rhs.at[zz, :, :, :, pl.ds(*lanes)]
        d = pltpu.make_async_remote_copy(ref, ref, s, rsem, device_id=dev, device_id_type=MESH)
        d.start()
        sent.append(d)

    def landed(zz, xx, lanes, rsem):
        ref = rhs.at[zz, :, xx, :, pl.ds(*lanes)] if xx is not None else rhs.at[zz, :, :, :, pl.ds(*lanes)]
        pltpu.make_async_copy(ref, ref, rsem).wait()

    up, down = trow_dev(at_z(1), x), trow_dev(at_z(-1), x)
    right, left = trow_dev(z, at_x(1)), trow_dev(z, at_x(-1))

    def a_z_send(t):
        lo, hi = (A, A) if t < 4 else (A1, A2)
        push(at_z(-(t - 1)), x, lo, za_s.at[0, t - 1], za_r.at[0, t - 1], up)
        push(at_z(t - 1), x, hi, za_s.at[1, t - 1], za_r.at[1, t - 1], down)

    def a_z_wait(t):
        lo, hi = (A, A) if t < 4 else (A1, A2)
        landed(at_z(-t), x, lo, za_r.at[0, t - 1])
        landed(at_z(t), x, hi, za_r.at[1, t - 1])

    def a_x_send(d):
        zz, e = at_z(d), d % NZ
        push(zz, x, A, xa_s.at[e, 0], xa_r.at[e, 0], right)
        push(zz, x, A, xa_s.at[e, 1], xa_r.at[e, 1], left)

    def a_x_forward(d):
        zz, e = at_z(d), d % NZ
        landed(zz, at_x(-1), A, xa_r.at[e, 0])
        push(zz, at_x(-1), A1, xa_s.at[e, 2], xa_r.at[e, 2], right)
        landed(zz, at_x(1), A, xa_r.at[e, 1])
        push(zz, at_x(1), A2, xa_s.at[e, 3], xa_r.at[e, 3], left)

    def a_x_last(d):
        zz, e = at_z(d), d % NZ
        landed(zz, at_x(2), A1, xa_r.at[e, 2])
        landed(zz, at_x(2), A2, xa_r.at[e, 3])

    def b_x_send():
        push(z, x, B, xb_s.at[0], xb_r.at[0], right)
        push(z, x, B, xb_s.at[1], xb_r.at[1], left)

    def b_x_forward():
        landed(z, at_x(-1), B, xb_r.at[0])
        push(z, at_x(-1), B1, xb_s.at[2], xb_r.at[2], right)
        landed(z, at_x(1), B, xb_r.at[1])
        push(z, at_x(1), B2, xb_s.at[3], xb_r.at[3], left)

    def b_x_last():
        landed(z, at_x(2), B1, xb_r.at[2])
        landed(z, at_x(2), B2, xb_r.at[3])

    def b_z_send(t):
        lo, hi = (B, B) if t < 4 else (B1, B2)
        push(at_z(-(t - 1)), None, lo, zb_s.at[0, t - 1], zb_r.at[0, t - 1], up)
        push(at_z(t - 1), None, hi, zb_s.at[1, t - 1], zb_r.at[1, t - 1], down)

    def b_z_wait(t):
        lo, hi = (B, B) if t < 4 else (B1, B2)
        landed(at_z(-t), None, lo, zb_r.at[0, t - 1])
        landed(at_z(t), None, hi, zb_r.at[1, t - 1])

    def mirror_send(d):
        for e in range(NX):
            if d == 0 and e == 0:
                continue
            q = at_z(d) * NX + at_x(e)
            pltpu.make_async_remote_copy(
                sb.at[q], rb.at[r], s1_send.at[0], s1_recv.at[r],
                device_id={"trow": q, "mode": m}, device_id_type=MESH,
            ).start()

    lane_group = lax.broadcasted_iota(jnp.int32, (16, 128), 1) // 16

    def mirror_regroup(d):
        kg = at_z(-d)
        for e in range(NX):
            if d == 0 and e == 0:
                continue
            q = kg * NX + at_x(-e)
            pltpu.make_async_copy(rb.at[q], rb.at[q], s1_recv.at[q]).wait()

        def one(ps, _):
            p, s = ps // 2, ps % 2
            tiles = [rb[kg * NX + k // 2, p, s, k % 2].astype(F32) for k in range(8)]
            for bit in (1, 2, 4):
                has = (lane_group // bit) % 2 == 1
                new = list(tiles)
                for k in range(8):
                    if k & bit:
                        continue
                    a, b = tiles[k], tiles[k + bit]
                    new[k] = jnp.where(has, pltpu.roll(b, 16 * bit, 1), a)
                    new[k + bit] = jnp.where(has, b, pltpu.roll(a, 128 - 16 * bit, 1))
                tiles = new
            for j in range(8):
                tb[kg, j, p, s] = tiles[j].astype(BF)
            return 0

        lax.fori_loop(0, 4, one, 0)

        def send(j, _):
            to = (m + 1 + j) % NMODE
            pltpu.make_async_remote_copy(
                tb.at[kg, to], mb.at[kg, m], s2_send.at[0], s2_recv.at[kg, m],
                device_id={"trow": r, "mode": to}, device_id_type=MESH,
            ).start()
            return 0

        lax.fori_loop(0, NMODE - 1, send, 0)
        mb[kg, m] = tb[kg, m]

    def sigma(d):
        kg = at_z(-d)

        def arrive(j, _):
            q = (m + 1 + j) % NMODE
            pltpu.make_async_copy(mb.at[kg, q], mb.at[kg, q], s2_recv.at[kg, q]).wait()
            return 0

        lax.fori_loop(0, NMODE - 1, arrive, 0)
        base = pl.multiple_of(kg * 256, 256)
        for s in range(2):
            hr = mb[kg, :, 0, s].reshape(128, 128).astype(F32)
            hi = mb[kg, :, 1, s].reshape(128, 128).astype(F32)
            qr, qi = sq[kg, s, 0], sq[kg, s, 1]
            sr = qr * hr - qi * hi
            si = qr * hi + qi * hr
            lo, hi_lanes = pl.ds(base, 128), pl.ds(base + 128, 128)
            lhs[pl.ds(128 * s, 128), lo] = sr.astype(BF)
            lhs[pl.ds(128 * s, 128), hi_lanes] = (-si).astype(BF)
            lhs[pl.ds(256 + 128 * s, 128), lo] = si.astype(BF)
            lhs[pl.ds(256 + 128 * s, 128), hi_lanes] = sr.astype(BF)

    def squares():
        def strengths(k, _):
            t = rt[k]
            row = dl[pl.ds(ds[t], 1), :]
            for s in range(2):
                live = jnp.where(t <= rt[2 * r + s], 1.0, 0.0).astype(F32)
                kb[s, k % 8, pl.ds(k // 8, 1), :] = row * live
            return 0

        lax.fori_loop(0, 64, strengths, 0)
        group8 = lax.broadcasted_iota(jnp.int32, (8, 128), 1) // 16
        for s in range(2):
            rows = jnp.zeros((8, 128), F32)
            for k in range(8):
                turned = pltpu.roll(kb[s, k], (16 * k + 128 - 16 * m) % 128, 1)
                rows = jnp.where(group8 == k, turned, rows)
            kb[s, 8] = rows
        cols = []
        for s in range(2):
            row = dl[pl.ds(ds[rt[2 * r + s]], 1), :]
            cols.append(jnp.broadcast_to(row, (128, 128)).T)

        def one(kg, _):
            for s in range(2):
                coupling = cols[s] * kb[s, 8, pl.ds(kg, 1), :]
                gr = sb[pl.ds(kg * NX, NX), 0, :, s].reshape(128, 128).astype(F32).T
                gi = sb[pl.ds(kg * NX, NX), 1, :, s].reshape(128, 128).astype(F32).T
                sq[kg, s, 0] = (gr * gr - gi * gi) * coupling
                sq[kg, s, 1] = (2.0 * gr * gi) * coupling
            return 0

        lax.fori_loop(0, NZ, one, 0)

    a_z_send(1)
    b_x_send()
    a_x_send(0)
    mirror_send(DZ[0])
    mirror_send(DZ[1])
    squares()

    b_x_forward()
    a_z_wait(1)
    a_z_send(2)
    a_x_send(-1)
    a_x_send(1)
    mirror_send(DZ[2])
    a_x_forward(0)

    b_x_last()
    b_z_send(1)
    a_z_wait(2)
    a_z_send(3)
    a_x_send(-2)
    a_x_send(2)
    mirror_send(DZ[3])
    mirror_regroup(DZ[0])
    a_x_forward(-1)
    a_x_forward(1)

    b_z_wait(1)
    b_z_send(2)
    a_z_wait(3)
    a_z_send(4)
    a_x_send(-3)
    a_x_send(3)
    mirror_send(DZ[4])
    mirror_regroup(DZ[1])
    a_x_forward(-2)
    a_x_forward(2)

    b_z_wait(2)
    b_z_send(3)
    a_z_wait(4)
    a_x_send(4)
    mirror_send(DZ[5])
    mirror_regroup(DZ[2])
    sigma(DZ[0])
    a_x_forward(-3)
    a_x_forward(3)

    b_z_wait(3)
    b_z_send(4)
    mirror_send(DZ[6])
    mirror_send(DZ[7])
    mirror_regroup(DZ[3])
    sigma(DZ[1])
    a_x_forward(4)

    for i in range(4, 8):
        mirror_regroup(DZ[i])
        sigma(DZ[i - 2])
    sigma(DZ[6])
    sigma(DZ[7])
    b_z_wait(4)
    for d in range(NZ):
        a_x_last(d)

    def core_copy(j):
        return pltpu.make_async_remote_copy(
            part.at[:, pl.ds(2 * j, 2), :, 1 - core], cb.at[:, pl.ds(2 * j, 2)], cx_s.at[j], cx_r.at[j],
            device_id={"trow": r, "mode": y * NCORE + 1 - core}, device_id_type=MESH,
        )

    def y_copy(j, e):
        to = (y + e) % NY
        return pltpu.make_async_remote_copy(
            red.at[:, pl.ds(2 * j, 2), to], yb.at[e - 1, :, pl.ds(2 * j, 2)], yx_s.at[j, e - 1], yx_r.at[j, e - 1],
            device_id={"trow": r, "mode": to * NCORE + core}, device_id_type=MESH,
        )

    def multiply(j):
        cols = rhs[:, :, :, :, pl.ds(256 * j, 256)].reshape(2048, 256)
        for h in range(2):
            acc = jnp.dot(lhs[pl.ds(256 * h, 256), :], cols, preferred_element_type=F32)
            for s in range(2):
                for n in range(2):
                    part[2 * h + s, 2 * j + n] = acc[128 * s : 128 * (s + 1), 128 * n : 128 * (n + 1)].reshape(
                        NY, NCORE, 16, 128
                    )
        core_copy(j).start()

    def core_sum(j):
        core_copy(j).wait_recv()
        here = pl.ds(2 * j, 2)
        red[:, here] = part[:, here, :, core] + cb[:, here]
        for e in (2, 1, 3):
            y_copy(j, e).start()

    def y_sum(j):
        for e in (2, 1, 3):
            y_copy(j, e).wait_recv()
        here = pl.ds(2 * j, 2)
        total = red[:, here, y] + (yb[1, :, here] + (yb[0, :, here] + yb[2, :, here]))
        out[:, :, here] = (total * SCALE).reshape(2, 2, 2, 16, 128)

    for j in range(4):
        multiply(j)
        if j >= 1:
            core_sum(j - 1)
    core_sum(3)
    for j in range(4):
        y_sum(j)

    for d in sent:
        d.wait_send()
    all_but_one = sb.at[pl.ds(0, NR - 1)]
    pltpu.make_async_copy(all_but_one, all_but_one, s1_send.at[0]).wait()
    all_but_own = tb.at[:, pl.ds(0, NMODE - 1)]
    pltpu.make_async_copy(all_but_own, all_but_own, s2_send.at[0]).wait()
    for j in range(4):
        core_copy(j).wait_send()
        for e in (2, 1, 3):
            y_copy(j, e).wait_send()


def body(g_hist, new_cols, row_time, drive_step, drive_levels):
    smem = pl.BlockSpec(memory_space=pltpu.SMEM)
    vmem = pl.BlockSpec(memory_space=pltpu.VMEM)
    dma = pltpu.SemaphoreType.DMA
    return pl.pallas_call(
        kernel,
        out_shape=jax.ShapeDtypeStruct((2, 2, 8, 16, 128), F32),
        in_specs=[smem, smem, vmem, vmem, vmem],
        out_specs=vmem,
        scratch_shapes=[
            pltpu.VMEM((NR, 2, 2, 2, 16, 128), BF),
            pltpu.VMEM((NR, 2, 2, 2, 16, 128), BF),
            pltpu.VMEM((NZ, NMODE, 2, 2, 16, 128), BF),
            pltpu.VMEM((NZ, NMODE, 2, 2, 16, 128), BF),
            pltpu.VMEM((NZ, 2, 2, 128, 128), F32),
            pltpu.VMEM((512, 2048), BF),
            pltpu.VMEM((NZ, 2, NX, 32, 1024), BF),
            pltpu.VMEM((4, 8, NY, NCORE, 16, 128), F32),
            pltpu.VMEM((4, 8, NY, 16, 128), F32),
            pltpu.VMEM((4, 8, NY, 16, 128), F32),
            pltpu.VMEM((3, 4, 8, 16, 128), F32),
            pltpu.VMEM((2, 9, 8, 128), F32),
            dma((1,)), dma((NR,)), dma((1,)), dma((NZ, NMODE)),
            dma((2, 4)), dma((2, 4)), dma((NZ, 4)), dma((NZ, 4)),
            dma((4,)), dma((4,)), dma((2, 4)), dma((2, 4)),
            dma((4,)), dma((4,)), dma((4, 3)), dma((4, 3)),
        ],
        compiler_params=pltpu.CompilerParams(
            collective_id=0, has_side_effects=True, vmem_limit_bytes=40 * 1024 * 1024
        ),
        cost_estimate=pl.CostEstimate(flops=2147483648, bytes_accessed=1600000, transcendentals=0),
    )(row_time, drive_step, drive_levels, g_hist, new_cols)


def solution(mesh):
    placed = (
        P(None, "trow", None, "mode", None),
        P(None, "trow", None, "mode", None),
        P(),
        P(),
        P(),
    )
    return jax.shard_map(
        body,
        mesh=mesh,
        in_specs=placed,
        out_specs=P(None, "trow", None, "mode", None),
        check_vma=False,
    )
```

time: 179 us -> 86.3 us (0.48); the launches traced: 176 us -> 86.1 us
  Pallas kernels: 0 us -> 81.3 us
  waiting for transfers between devices: 71 us -> 0 us
  local copies, waits for them, and re-layouts: 53.2 us -> 4.84 us
  starting transfers between devices: 20 us -> 0 us
  between operations: 13.6 us -> 0.01 us
  other arithmetic: 13 us -> 0 us
  matrix products: 5 us -> 0 us
    pallas_call x0 -> x1, Pallas kernels: none -> 81.3 us  [body(): pl.pallas_call(kernel, out_shape=jax.ShapeDtypeStruct((2, 2, 8, 16, 128),...]
    all_to_all x2 -> x0, waiting for transfers between devices: 41.8 us -> none  [the longest x1 28.7 us: body(): lax.all_to_all(outgoing, 'trow', split_axis=1, concat_axis=1, tiled=True)]
    reduce_scatter x1 -> x0, waiting for transfers between devices: 29.2 us -> none  [body(): lax.psum_scatter(partials, 'mode', scatter_dimension=3, tiled=True)]
    convert_element_type x2 -> x0, local copies, waits for them, and re-layouts: 26.2 us -> none  [body(): mirror = jnp.transpose(incoming, (0, 2, 1, 3, 4)).astype(jnp.float32)]
    all_to_all x2 -> x0, starting transfers between devices: 20 us -> none  [the longest x1 11.9 us: body(): lax.all_to_all(outgoing, 'trow', split_axis=1, concat_axis=1, tiled=True)]
    unnamed x17 -> x11, local copies, waits for them, and re-layouts: 14.8 us -> 4.84 us
    all_to_all x2 -> x0, local copies, waits for them, and re-layouts: 9.77 us -> none  [the longest x1 6.83 us: body(): lax.all_to_all(outgoing, 'trow', split_axis=1, concat_axis=1, tiled=True)]
    convert_element_type x3 -> x0, other arithmetic: 8.69 us -> none  [the longest x1 4.36 us: body(): mirror = jnp.transpose(incoming, (0, 2, 1, 3, 4)).astype(jnp.float32)]
  transfers between devices with their start and end apart: 4 -> 0, of which waited for: 3 -> 0; matrix products, arithmetic and copies ran while one was open for 35% -> 0% of each run, Pallas kernels for 0% -> 0%
where the time goes in v1:
time: 86.3 us; the launch traced here: 86.1 us
  Pallas kernels  81.3 us (94%)
  local copies, waits for them, and re-layouts  4.84 us (6%)
    pallas_call x1, Pallas kernels, body(): pl.pallas_call(kernel, out_shape=jax.ShapeDtypeStruct((2, 2, 8, 16, 128),...  81.3 us
    unnamed x11, local copies, waits for them, and re-layouts  4.84 us

profile of v1, /device:TPU:1, one launch (start us, length us, event | category | flops | bytes accessed | tf_op | source)
XLA Modules:
  0.0 86.1 jit_solution(3009592522760009931)
XLA Ops:
  0.0 0.0 copy-start
  0.0 1.2 %copy-done = bf16[2,2,64,16,128]{4,3,2,1,0:T(8,128)(2,1)S(1)} copy-done((bf16[2,2,64,16,128]{4,3,2,1,0:T(8,128)(2,1)S(1)}, bf16[2,2,64,16,128]{4,3,2,1,0:T(8,128)(2,1)}, u32[]{:S(2)}) %copy-start) | copy-done | bytes 1048600
  1.2 0.0 copy-start.1
  1.2 0.9 %copy-done.1 = bf16[2,2,8,16,128]{4,3,2,1,0:T(8,128)(2,1)S(1)} copy-done((bf16[2,2,8,16,128]{4,3,2,1,0:T(8,128)(2,1)S(1)}, bf16[2,2,8,16,128]{4,3,2,1,0:T(8,128)(2,1)}, u32[]{:S(2)}) %copy-start.1) | copy-done | bytes 131096
  2.1 0.0 copy-start.2
  2.1 0.7 copy-done.2
  2.8 0.0 copy-start.3
  2.8 0.7 copy-done.3
  3.5 0.0 copy-start.4
  3.5 0.7 copy-done.4
  4.1 81.3 %shard_map.55 = f32[2,2,8,16,128]{4,3,2,1,0:T(8,128)S(1)} custom-call(s32[64]{0:T(128)S(1)} %copy-done.3, s32[64]{0:T(128)S(1)} %copy-done.4, f32[16,128]{1,0:T(8,128)S(1)} %copy-done.2, bf16[2,2,64,16,128]{4,3,2,1,0:T(8,128)(2,1)S(1)} %copy-done, bf16[2,2,8,16,128]{4,3,2,1,0:T(8,128)(2,1)S(1)} %copy-done.1), custom_call_target="tpu_custom_call" | custom-call | flops 2147483648 | bytes 1600000 | tf_op jit(solution)/shard_map/pallas_call | solution.py:370
  85.4 0.7 copy.7
Async XLA Ops:
  0.0 1.2 %copy-start = (bf16[2,2,64,16,128]{4,3,2,1,0:T(8,128)(2,1)S(1)}, bf16[2,2,64,16,128]{4,3,2,1,0:T(8,128)(2,1)}, u32[]{:S(2)}) copy-start(bf16[2,2,64,16,128]{4,3,2,1,0:T(8,128)(2,1)} %g.1) | copy-start | bytes 3145732
  1.2 0.9 %copy-start.1 = (bf16[2,2,8,16,128]{4,3,2,1,0:T(8,128)(2,1)S(1)}, bf16[2,2,8,16,128]{4,3,2,1,0:T(8,128)(2,1)}, u32[]{:S(2)}) copy-start(bf16[2,2,8,16,128]{4,3,2,1,0:T(8,128)(2,1)} %c.1) | copy-start | bytes 393220
  2.1 0.7 copy-start.2
  2.8 0.7 copy-start.3
  3.5 0.7 copy-start.4

commit v2 on v1

v2 whole, which is shorter than its diff:
```python
import jax
import jax.numpy as jnp
from jax import lax
from jax.experimental import pallas as pl
from jax.experimental.pallas import tpu as pltpu
from jax.sharding import PartitionSpec as P

NZ, NX, NY, NCORE = 8, 4, 4, 2
NR, NMODE = NZ * NX, NY * NCORE
BF, F32 = jnp.bfloat16, jnp.float32
MESH = pl.DeviceIdType.MESH

CHUNK = ((3, 1), (3, 1))
PIECE = (4, 4)
YT = BF

SCALE = 8.0 / 64


def lanes(chunk, which):
    first = sum(a + b for a, b in CHUNK[:chunk]) + (CHUNK[chunk][0] if which else 0)
    return 128 * first, 128 * CHUNK[chunk][which]


A = [lanes(i, 0) for i in range(len(CHUNK))]
B = [lanes(i, 1) for i in range(len(CHUNK))]
FIRST = [sum(PIECE[:i]) for i in range(len(PIECE))]


def kernel(
    rt_hbm, ds_hbm, dl_hbm, g_hbm, c_hbm, out,
    rt, ds, dl, g, c,
    sb, rb, tb, mb, sq, lhs, rhs, part, cb, red, yb, kb,
    in_sem, s1_send, s1_recv, s2_send, s2_recv,
    za_s, za_r, xa_s, xa_r, xb_s, xb_r, zb_s, zb_r,
    cx_s, cx_r, yx_s, yx_r,
):
    loads = [
        pltpu.make_async_copy(src, dst, in_sem.at[i])
        for i, (src, dst) in enumerate(((c_hbm, c), (rt_hbm, rt), (g_hbm, g), (ds_hbm, ds), (dl_hbm, dl)))
    ]
    for load in loads:
        load.start()
    r = lax.axis_index("trow")
    m = lax.axis_index("mode")
    z, x = r // NX, r % NX
    y, core = m // NCORE, m % NCORE

    def at_z(d):
        return (z + d + NZ) % NZ

    def at_x(d):
        return (x + d + NX) % NX

    def trow_dev(zz, xx):
        return {"trow": zz * NX + xx, "mode": m}

    bar = pltpu.get_barrier_semaphore()

    def greet_trow(j, _):
        pl.semaphore_signal(bar, inc=1, device_id={"trow": (r + 1 + j) % NR, "mode": m}, device_id_type=MESH)
        return 0

    def greet_mode(j, _):
        pl.semaphore_signal(bar, inc=1, device_id={"trow": r, "mode": (m + 1 + j) % NMODE}, device_id_type=MESH)
        return 0

    lax.fori_loop(0, NR - 1, greet_trow, 0)
    lax.fori_loop(0, NMODE - 1, greet_mode, 0)

    loads[0].wait()
    for p in range(2):
        for k in range(2):
            for n in range(8):
                rhs[z, p, x, pl.ds(16 * k, 16), pl.ds(128 * n, 128)] = c[p, k, n]

    def fill():
        loads[1].wait()
        loads[2].wait()

        def one(q, _):
            for i in range(2):
                t = rt[2 * q + i]
                for p in range(2):
                    for o in range(2):
                        sb[q, p, i, o] = g[p, o, t]
            return 0

        lax.fori_loop(0, NR, one, 0)
        rb[r] = sb[r]

    pl.semaphore_wait(bar, NR - 1 + NMODE - 1)

    sent = []

    def block(zz, xx, lanes, half):
        h = slice(None) if half is None else half
        return rhs.at[zz, h, slice(None) if xx is None else xx, :, pl.ds(*lanes)]

    def push(zz, xx, lanes, half, ssem, rsem, dev):
        ref = block(zz, xx, lanes, half)
        d = pltpu.make_async_remote_copy(ref, ref, ssem, rsem, device_id=dev, device_id_type=MESH)
        d.start()
        sent.append(d)

    def landed(zz, xx, lanes, half, rsem):
        ref = block(zz, xx, lanes, half)
        pltpu.make_async_copy(ref, ref, rsem).wait()

    up, down = trow_dev(at_z(1), x), trow_dev(at_z(-1), x)
    right, left = trow_dev(z, at_x(1)), trow_dev(z, at_x(-1))

    def z_send(t, xx, lanes, ssem, rsem):
        lo, hi = (None, None) if t < 4 else (0, 1)
        push(at_z(-(t - 1)), xx, lanes, lo, ssem.at[0, t - 1], rsem.at[0, t - 1], up)
        push(at_z(t - 1), xx, lanes, hi, ssem.at[1, t - 1], rsem.at[1, t - 1], down)

    def z_wait(t, xx, lanes, rsem):
        lo, hi = (None, None) if t < 4 else (0, 1)
        landed(at_z(-t), xx, lanes, lo, rsem.at[0, t - 1])
        landed(at_z(t), xx, lanes, hi, rsem.at[1, t - 1])

    def x_send(d, lanes, ssem, rsem):
        push(at_z(d), x, lanes, None, ssem.at[0], rsem.at[0], right)
        push(at_z(d), x, lanes, None, ssem.at[1], rsem.at[1], left)

    def x_forward(d, lanes, ssem, rsem):
        zz = at_z(d)
        landed(zz, at_x(-1), lanes, None, rsem.at[0])
        push(zz, at_x(-1), lanes, 0, ssem.at[2], rsem.at[2], right)
        landed(zz, at_x(1), lanes, None, rsem.at[1])
        push(zz, at_x(1), lanes, 1, ssem.at[3], rsem.at[3], left)

    def x_last(d, lanes, rsem):
        zz = at_z(d)
        landed(zz, at_x(2), lanes, 0, rsem.at[2])
        landed(zz, at_x(2), lanes, 1, rsem.at[3])

    def za(ch):
        return za_s.at[ch], za_r.at[ch]

    def xa(ch, d):
        return xa_s.at[ch, d % NZ], xa_r.at[ch, d % NZ]

    def hop(ch, t):
        if t > 0:
            z_wait(t, x, A[ch], za(ch)[1])
        if t < 4:
            z_send(t + 1, x, A[ch], *za(ch))
        for d in {0: (0,), 4: (4,)}.get(t, (-t, t)):
            x_send(d, A[ch], *xa(ch, d))

    def forward(ch, t):
        for d in {0: (0,), 4: (4,)}.get(t, (-t, t)):
            x_forward(d, A[ch], *xa(ch, d))

    def last(ch):
        for d in range(NZ):
            x_last(d, A[ch], xa(ch, d)[1])

    def x_first(ch, t):
        xb = (xb_s.at[ch], xb_r.at[ch])
        zb = (zb_s.at[ch], zb_r.at[ch])
        if t == 0:
            x_send(0, B[ch], *xb)
        if t == 1:
            x_forward(0, B[ch], *xb)
        if t == 2:
            x_last(0, B[ch], xb[1])
        if t >= 3:
            z_wait(t - 2, None, B[ch], zb[1])
        if 2 <= t <= 5:
            z_send(t - 1, None, B[ch], *zb)

    def mirror_send(d, e):
        q = at_z(d) * NX + at_x(e)
        pltpu.make_async_remote_copy(
            sb.at[q], rb.at[r], s1_send.at[0], s1_recv.at[r],
            device_id={"trow": q, "mode": m}, device_id_type=MESH,
        ).start()

    lane_group = lax.broadcasted_iota(jnp.int32, (16, 128), 1) // 16

    def mirror_regroup(d):
        kg = at_z(-d)
        for e in range(NX):
            if d == 0 and e == 0:
                continue
            q = kg * NX + at_x(-e)
            pltpu.make_async_copy(rb.at[q], rb.at[q], s1_recv.at[q]).wait()

        def one(ps, _):
            p, s = ps // 2, ps % 2
            tiles = [rb[kg * NX + k // 2, p, s, k % 2].astype(F32) for k in range(8)]
            for bit in (1, 2, 4):
                has = (lane_group // bit) % 2 == 1
                new = list(tiles)
                for k in range(8):
                    if k & bit:
                        continue
                    a, b = tiles[k], tiles[k + bit]
                    new[k] = jnp.where(has, pltpu.roll(b, 16 * bit, 1), a)
                    new[k + bit] = jnp.where(has, b, pltpu.roll(a, 128 - 16 * bit, 1))
                tiles = new
            for j in range(8):
                tb[kg, j, p, s] = tiles[j].astype(BF)
            return 0

        for ps in range(4):
            one(ps, 0)

        def send(j, _):
            to = (m + 1 + j) % NMODE
            pltpu.make_async_remote_copy(
                tb.at[kg, to], mb.at[kg, m], s2_send.at[0], s2_recv.at[kg, m],
                device_id={"trow": r, "mode": to}, device_id_type=MESH,
            ).start()
            return 0

        lax.fori_loop(0, NMODE - 1, send, 0)
        mb[kg, m] = tb[kg, m]

    def sigma(d):
        kg = at_z(-d)

        def arrive(j, _):
            q = (m + 1 + j) % NMODE
            pltpu.make_async_copy(mb.at[kg, q], mb.at[kg, q], s2_recv.at[kg, q]).wait()
            return 0

        lax.fori_loop(0, NMODE - 1, arrive, 0)
        base = pl.multiple_of(kg * 256, 256)
        for s in range(2):
            hr = mb[kg, :, 0, s].reshape(128, 128).astype(F32)
            hi = mb[kg, :, 1, s].reshape(128, 128).astype(F32)
            qr, qi = sq[kg, s, 0], sq[kg, s, 1]
            sr = qr * hr - qi * hi
            si = qr * hi + qi * hr
            lo, hi_lanes = pl.ds(base, 128), pl.ds(base + 128, 128)
            lhs[pl.ds(128 * s, 128), lo] = sr.astype(BF)
            lhs[pl.ds(128 * s, 128), hi_lanes] = (-si).astype(BF)
            lhs[pl.ds(256 + 128 * s, 128), lo] = si.astype(BF)
            lhs[pl.ds(256 + 128 * s, 128), hi_lanes] = sr.astype(BF)

    def squares():
        loads[3].wait()
        loads[4].wait()

        def strengths(k, _):
            t = rt[k]
            row = dl[pl.ds(ds[t], 1), :]
            for s in range(2):
                live = jnp.where(t <= rt[2 * r + s], 1.0, 0.0).astype(F32)
                kb[s, k % 8, pl.ds(k // 8, 1), :] = row * live
            return 0

        lax.fori_loop(0, 64, strengths, 0)
        group8 = lax.broadcasted_iota(jnp.int32, (8, 128), 1) // 16
        for s in range(2):
            rows = jnp.zeros((8, 128), F32)
            for k in range(8):
                turned = pltpu.roll(kb[s, k], (16 * k + 128 - 16 * m) % 128, 1)
                rows = jnp.where(group8 == k, turned, rows)
            kb[s, 8] = rows
        cols = []
        for s in range(2):
            row = dl[pl.ds(ds[rt[2 * r + s]], 1), :]
            cols.append(jnp.broadcast_to(row, (128, 128)).T)

        def one(kg, _):
            for s in range(2):
                coupling = cols[s] * kb[s, 8, pl.ds(kg, 1), :]
                gr = sb[pl.ds(kg * NX, NX), 0, :, s].reshape(128, 128).astype(F32).T
                gi = sb[pl.ds(kg * NX, NX), 1, :, s].reshape(128, 128).astype(F32).T
                sq[kg, s, 0] = (gr * gr - gi * gi) * coupling
                sq[kg, s, 1] = (2.0 * gr * gi) * coupling
            return 0

        lax.fori_loop(0, NZ, one, 0)

    def core_copy(j):
        here = pl.ds(FIRST[j], PIECE[j])
        return pltpu.make_async_remote_copy(
            part.at[:, here, :, 1 - core], cb.at[:, here], cx_s.at[j], cx_r.at[j],
            device_id={"trow": r, "mode": y * NCORE + 1 - core}, device_id_type=MESH,
        )

    def y_copy(j, e):
        here = pl.ds(FIRST[j], PIECE[j])
        to = (y + e) % NY
        return pltpu.make_async_remote_copy(
            red.at[:, here, to], yb.at[e - 1, :, here], yx_s.at[j, e - 1], yx_r.at[j, e - 1],
            device_id={"trow": r, "mode": to * NCORE + core}, device_id_type=MESH,
        )

    def multiply(j):
        n = FIRST[j]
        while n < FIRST[j] + PIECE[j]:
            width = min(2, FIRST[j] + PIECE[j] - n)
            cols = rhs[:, :, :, :, 128 * n : 128 * (n + width)].reshape(2048, 128 * width)
            for h in range(2):
                acc = jnp.dot(lhs[pl.ds(256 * h, 256), :], cols, preferred_element_type=F32)
                for s in range(2):
                    for w in range(width):
                        part[2 * h + s, n + w] = acc[128 * s : 128 * (s + 1), 128 * w : 128 * (w + 1)].reshape(
                            NY, NCORE, 16, 128
                        )
            n += width
        core_copy(j).start()

    def core_sum(j):
        core_copy(j).wait_recv()
        here = pl.ds(FIRST[j], PIECE[j])
        red[:, here] = (part[:, here, :, core] + cb[:, here]).astype(YT)
        for e in (2, 1, 3):
            y_copy(j, e).start()

    def y_sum(j):
        for e in (2, 1, 3):
            y_copy(j, e).wait_recv()
        here = pl.ds(FIRST[j], PIECE[j])
        own = part[:, here, y, core] + cb[:, here, y]
        total = own + (yb[1, :, here].astype(F32) + (yb[0, :, here].astype(F32) + yb[2, :, here].astype(F32)))
        out[:, :, here] = (total * SCALE).reshape(2, 2, PIECE[j], 16, 128)

    hop(1, 0)
    hop(0, 0)
    fill()
    mirror_send(5, 0)
    mirror_send(4, 0)
    mirror_send(1, 2)
    mirror_send(4, 2)
    mirror_send(1, 0)
    mirror_send(1, 1)
    mirror_send(7, 3)
    x_first(0, 0)
    mirror_send(7, 0)
    mirror_send(4, 3)
    mirror_send(3, 1)
    mirror_send(6, 0)
    hop(1, 1)
    hop(0, 1)
    x_first(1, 0)
    mirror_send(0, 1)
    mirror_send(0, 2)
    squares()
    mirror_send(4, 1)
    x_first(1, 1)
    mirror_send(3, 0)
    x_first(0, 1)
    forward(1, 1)
    mirror_send(5, 2)
    mirror_send(3, 3)
    hop(1, 2)
    mirror_send(6, 2)
    forward(0, 0)
    mirror_send(7, 1)
    mirror_send(1, 3)
    mirror_send(7, 2)
    hop(0, 2)
    mirror_regroup(4)
    x_first(1, 2)
    mirror_send(0, 3)
    mirror_send(6, 1)
    mirror_send(2, 0)
    mirror_send(3, 2)
    hop(1, 3)
    mirror_send(2, 2)
    x_first(0, 2)
    mirror_send(5, 1)
    mirror_send(6, 3)
    mirror_regroup(1)
    x_first(1, 3)
    forward(0, 2)
    mirror_regroup(7)
    mirror_send(5, 3)
    sigma(4)
    mirror_regroup(0)
    mirror_send(2, 1)
    forward(1, 2)
    mirror_send(2, 3)
    mirror_regroup(3)
    hop(0, 3)
    x_first(0, 3)
    forward(1, 0)
    forward(1, 3)
    sigma(3)
    hop(1, 4)
    x_first(1, 4)
    forward(0, 1)
    mirror_regroup(6)
    sigma(1)
    mirror_regroup(2)
    sigma(0)
    hop(0, 4)
    x_first(0, 4)
    mirror_regroup(5)
    forward(1, 4)
    sigma(7)
    x_first(1, 5)
    sigma(2)
    forward(0, 3)
    sigma(6)
    last(1)
    forward(0, 4)
    x_first(0, 5)
    x_first(1, 6)
    sigma(5)
    multiply(1)
    x_first(0, 6)
    last(0)
    multiply(0)
    core_sum(1)
    core_sum(0)
    y_sum(1)
    y_sum(0)

    for d in sent:
        d.wait_send()
    all_but_one = sb.at[pl.ds(0, NR - 1)]
    pltpu.make_async_copy(all_but_one, all_but_one, s1_send.at[0]).wait()
    all_but_own = tb.at[:, pl.ds(0, NMODE - 1)]
    pltpu.make_async_copy(all_but_own, all_but_own, s2_send.at[0]).wait()
    for j in range(len(PIECE)):
        core_copy(j).wait_send()
        for e in (2, 1, 3):
            y_copy(j, e).wait_send()


def body(g_hist, new_cols, row_time, drive_step, drive_levels):
    hbm = pl.BlockSpec(memory_space=pltpu.HBM)
    vmem = pl.BlockSpec(memory_space=pltpu.VMEM)
    dma = pltpu.SemaphoreType.DMA
    return pl.pallas_call(
        kernel,
        out_shape=jax.ShapeDtypeStruct((2, 2, 8, 16, 128), F32),
        in_specs=[hbm] * 5,
        out_specs=vmem,
        scratch_shapes=[
            pltpu.SMEM((64,), jnp.int32),
            pltpu.SMEM((64,), jnp.int32),
            pltpu.VMEM((16, 128), F32),
            pltpu.VMEM((2, 2, 64, 16, 128), BF),
            pltpu.VMEM((2, 2, 8, 16, 128), BF),
            pltpu.VMEM((NR, 2, 2, 2, 16, 128), BF),
            pltpu.VMEM((NR, 2, 2, 2, 16, 128), BF),
            pltpu.VMEM((NZ, NMODE, 2, 2, 16, 128), BF),
            pltpu.VMEM((NZ, NMODE, 2, 2, 16, 128), BF),
            pltpu.VMEM((NZ, 2, 2, 128, 128), F32),
            pltpu.VMEM((512, 2048), BF),
            pltpu.VMEM((NZ, 2, NX, 32, 1024), BF),
            pltpu.VMEM((4, 8, NY, NCORE, 16, 128), F32),
            pltpu.VMEM((4, 8, NY, 16, 128), F32),
            pltpu.VMEM((4, 8, NY, 16, 128), YT),
            pltpu.VMEM((3, 4, 8, 16, 128), YT),
            pltpu.VMEM((2, 9, 8, 128), F32),
            dma((5,)), dma((1,)), dma((NR,)), dma((1,)), dma((NZ, NMODE)),
            dma((len(CHUNK), 2, 4)), dma((len(CHUNK), 2, 4)), dma((len(CHUNK), NZ, 4)), dma((len(CHUNK), NZ, 4)),
            dma((len(CHUNK), 4)), dma((len(CHUNK), 4)), dma((len(CHUNK), 2, 4)), dma((len(CHUNK), 2, 4)),
            dma((len(PIECE),)), dma((len(PIECE),)), dma((len(PIECE), 3)), dma((len(PIECE), 3)),
        ],
        compiler_params=pltpu.CompilerParams(
            collective_id=0, has_side_effects=True, vmem_limit_bytes=58 * 1024 * 1024
        ),
        cost_estimate=pl.CostEstimate(flops=2147483648, bytes_accessed=1600000, transcendentals=0),
    )(row_time, drive_step, drive_levels, g_hist, new_cols)


def solution(mesh):
    placed = (
        P(None, "trow", None, "mode", None),
        P(None, "trow", None, "mode", None),
        P(),
        P(),
        P(),
    )
    return jax.shard_map(
        body,
        mesh=mesh,
        in_specs=placed,
        out_specs=P(None, "trow", None, "mode", None),
        check_vma=False,
    )
```

time: 86.3 us -> 72.4 us (0.84)
  Pallas kernels: 81.3 us -> 70.6 us
  local copies, waits for them, and re-layouts: 4.84 us -> 1.67 us
    pallas_call x1, Pallas kernels: 81.3 us -> 70.6 us  [body(): pl.pallas_call(kernel, out_shape=jax.ShapeDtypeStruct((2, 2, 8, 16, 128),...]
    unnamed x11 -> x1, local copies, waits for them, and re-layouts: 4.84 us -> 1.67 us
where the time goes in v2:
time: 72.4 us; the launch traced here: 72.3 us
  Pallas kernels  70.6 us (98%)
  local copies, waits for them, and re-layouts  1.67 us (2%)
    pallas_call x1, Pallas kernels, body(): pl.pallas_call(kernel, out_shape=jax.ShapeDtypeStruct((2, 2, 8, 16, 128),...  70.6 us
    unnamed x1, local copies, waits for them, and re-layouts  1.67 us

profile of v2, /device:TPU:1, one launch (start us, length us, event | category | flops | bytes accessed | tf_op | source)
XLA Modules:
  0.0 72.3 jit_solution(14543296884423546527)
XLA Ops:
  0.0 70.6 %shard_map.55 = f32[2,2,8,16,128]{4,3,2,1,0:T(8,128)} custom-call(s32[64]{0:T(128)} %rt_hbm.1, s32[64]{0:T(128)} %ds_hbm.1, f32[16,128]{1,0:T(8,128)} %dl_hbm.1, bf16[2,2,64,16,128]{4,3,2,1,0:T(8,128)(2,1)} %g_hbm.1, bf16[2,2,8,16,128]{4,3,2,1,0:T(8,128)(2,1)} %c_hbm.1), custom_call_target="tpu_custom_call" | custom-call | flops 2147483648 | bytes 1600000 | tf_op jit(solution)/shard_map/pallas_call | solution.py:434
  70.6 1.7 %copy.7 = f32[2,2,8,16,128]{4,3,2,1,0:T(8,128)} copy(f32[2,2,8,16,128]{4,3,2,1,0:T(8,128)} %shard_map.55) | data formatting | bytes 524288

commit v3 on v2

--- a/solution.py
+++ b/solution.py
@@ -11,40 +11,42 @@
 MESH = pl.DeviceIdType.MESH
 
 CHUNK = ((3, 1), (3, 1))
-PIECE = (4, 4)
+PIECE = (2, 2, 2, 2)
 YT = BF
 
 SCALE = 8.0 / 64
 
 
-def lanes(chunk, which):
+def blocks(chunk, which):
     first = sum(a + b for a, b in CHUNK[:chunk]) + (CHUNK[chunk][0] if which else 0)
-    return 128 * first, 128 * CHUNK[chunk][which]
-
-
-A = [lanes(i, 0) for i in range(len(CHUNK))]
-B = [lanes(i, 1) for i in range(len(CHUNK))]
+    return first, CHUNK[chunk][which]
+
+
+A = [blocks(i, 0) for i in range(len(CHUNK))]
+B = [blocks(i, 1) for i in range(len(CHUNK))]
 FIRST = [sum(PIECE[:i]) for i in range(len(PIECE))]
 
 
 def kernel(
     rt_hbm, ds_hbm, dl_hbm, g_hbm, c_hbm, out,
-    rt, ds, dl, g, c,
+    rt, ds, dl, g,
     sb, rb, tb, mb, sq, lhs, rhs, part, cb, red, yb, kb,
     in_sem, s1_send, s1_recv, s2_send, s2_recv,
     za_s, za_r, xa_s, xa_r, xb_s, xb_r, zb_s, zb_r,
     cx_s, cx_r, yx_s, yx_r,
 ):
-    loads = [
-        pltpu.make_async_copy(src, dst, in_sem.at[i])
-        for i, (src, dst) in enumerate(((c_hbm, c), (rt_hbm, rt), (g_hbm, g), (ds_hbm, ds), (dl_hbm, dl)))
-    ]
-    for load in loads:
-        load.start()
     r = lax.axis_index("trow")
     m = lax.axis_index("mode")
     z, x = r // NX, r % NX
     y, core = m // NCORE, m % NCORE
+    loads = [
+        pltpu.make_async_copy(src, dst, in_sem.at[i])
+        for i, (src, dst) in enumerate(
+            ((g_hbm, g), (rt_hbm, rt), (c_hbm, rhs.at[z, :, x]), (ds_hbm, ds), (dl_hbm, dl))
+        )
+    ]
+    for load in loads:
+        load.start()
 
     def at_z(d):
         return (z + d + NZ) % NZ
@@ -68,15 +70,9 @@
     lax.fori_loop(0, NR - 1, greet_trow, 0)
     lax.fori_loop(0, NMODE - 1, greet_mode, 0)
 
-    loads[0].wait()
-    for p in range(2):
-        for k in range(2):
-            for n in range(8):
-                rhs[z, p, x, pl.ds(16 * k, 16), pl.ds(128 * n, 128)] = c[p, k, n]
-
     def fill():
-        loads[1].wait()
-        loads[2].wait()
+        for load in loads[:3]:
+            load.wait()
 
         def one(q, _):
             for i in range(2):
@@ -93,48 +89,50 @@
 
     sent = []
 
-    def block(zz, xx, lanes, half):
+    def block(zz, xx, cols, half):
         h = slice(None) if half is None else half
-        return rhs.at[zz, h, slice(None) if xx is None else xx, :, pl.ds(*lanes)]
-
-    def push(zz, xx, lanes, half, ssem, rsem, dev):
-        ref = block(zz, xx, lanes, half)
-        d = pltpu.make_async_remote_copy(ref, ref, ssem, rsem, device_id=dev, device_id_type=MESH)
+        return rhs.at[zz, h, slice(None) if xx is None else xx, :, pl.ds(*cols)]
+
+    def push(zz, xx, cols, half, ssem, rsem, dev, own=False):
+        dst = block(zz, xx, cols, half)
+        src = c_hbm.at[:, :, pl.ds(*cols)] if own else dst
+        d = pltpu.make_async_remote_copy(src, dst, ssem, rsem, device_id=dev, device_id_type=MESH)
         d.start()
         sent.append(d)
 
-    def landed(zz, xx, lanes, half, rsem):
-        ref = block(zz, xx, lanes, half)
+    def landed(zz, xx, cols, half, rsem):
+        ref = block(zz, xx, cols, half)
         pltpu.make_async_copy(ref, ref, rsem).wait()
 
     up, down = trow_dev(at_z(1), x), trow_dev(at_z(-1), x)
     right, left = trow_dev(z, at_x(1)), trow_dev(z, at_x(-1))
 
-    def z_send(t, xx, lanes, ssem, rsem):
+    def z_send(t, xx, cols, ssem, rsem):
         lo, hi = (None, None) if t < 4 else (0, 1)
-        push(at_z(-(t - 1)), xx, lanes, lo, ssem.at[0, t - 1], rsem.at[0, t - 1], up)
-        push(at_z(t - 1), xx, lanes, hi, ssem.at[1, t - 1], rsem.at[1, t - 1], down)
-
-    def z_wait(t, xx, lanes, rsem):
+        own = t == 1 and xx is not None
+        push(at_z(-(t - 1)), xx, cols, lo, ssem.at[0, t - 1], rsem.at[0, t - 1], up, own)
+        push(at_z(t - 1), xx, cols, hi, ssem.at[1, t - 1], rsem.at[1, t - 1], down, own)
+
+    def z_wait(t, xx, cols, rsem):
         lo, hi = (None, None) if t < 4 else (0, 1)
-        landed(at_z(-t), xx, lanes, lo, rsem.at[0, t - 1])
-        landed(at_z(t), xx, lanes, hi, rsem.at[1, t - 1])
-
-    def x_send(d, lanes, ssem, rsem):
-        push(at_z(d), x, lanes, None, ssem.at[0], rsem.at[0], right)
-        push(at_z(d), x, lanes, None, ssem.at[1], rsem.at[1], left)
-
-    def x_forward(d, lanes, ssem, rsem):
+        landed(at_z(-t), xx, cols, lo, rsem.at[0, t - 1])
+        landed(at_z(t), xx, cols, hi, rsem.at[1, t - 1])
+
+    def x_send(d, cols, ssem, rsem):
+        push(at_z(d), x, cols, None, ssem.at[0], rsem.at[0], right, d == 0)
+        push(at_z(d), x, cols, None, ssem.at[1], rsem.at[1], left, d == 0)
+
+    def x_forward(d, cols, ssem, rsem):
         zz = at_z(d)
-        landed(zz, at_x(-1), lanes, None, rsem.at[0])
-        push(zz, at_x(-1), lanes, 0, ssem.at[2], rsem.at[2], right)
-        landed(zz, at_x(1), lanes, None, rsem.at[1])
-        push(zz, at_x(1), lanes, 1, ssem.at[3], rsem.at[3], left)
-
-    def x_last(d, lanes, rsem):
+        landed(zz, at_x(-1), cols, None, rsem.at[0])
+        push(zz, at_x(-1), cols, 0, ssem.at[2], rsem.at[2], right)
+        landed(zz, at_x(1), cols, None, rsem.at[1])
+        push(zz, at_x(1), cols, 1, ssem.at[3], rsem.at[3], left)
+
+    def x_last(d, cols, rsem):
         zz = at_z(d)
-        landed(zz, at_x(2), lanes, 0, rsem.at[2])
-        landed(zz, at_x(2), lanes, 1, rsem.at[3])
+        landed(zz, at_x(2), cols, 0, rsem.at[2])
+        landed(zz, at_x(2), cols, 1, rsem.at[3])
 
     def za(ch):
         return za_s.at[ch], za_r.at[ch]
@@ -191,7 +189,7 @@
 
         def one(ps, _):
             p, s = ps // 2, ps % 2
-            tiles = [rb[kg * NX + k // 2, p, s, k % 2].astype(F32) for k in range(8)]
+            tiles = [rb[kg * NX + k // 2, p, s, k % 2] for k in range(8)]
             for bit in (1, 2, 4):
                 has = (lane_group // bit) % 2 == 1
                 new = list(tiles)
@@ -203,7 +201,7 @@
                     new[k + bit] = jnp.where(has, b, pltpu.roll(a, 128 - 16 * bit, 1))
                 tiles = new
             for j in range(8):
-                tb[kg, j, p, s] = tiles[j].astype(BF)
+                tb[kg, j, p, s] = tiles[j]
             return 0
 
         for ps in range(4):
@@ -294,18 +292,29 @@
         )
 
     def multiply(j):
-        n = FIRST[j]
-        while n < FIRST[j] + PIECE[j]:
-            width = min(2, FIRST[j] + PIECE[j] - n)
-            cols = rhs[:, :, :, :, 128 * n : 128 * (n + width)].reshape(2048, 128 * width)
-            for h in range(2):
-                acc = jnp.dot(lhs[pl.ds(256 * h, 256), :], cols, preferred_element_type=F32)
+        def product(n, width):
+            cols = jnp.concatenate([rhs[:, :, :, :, n + w].reshape(2048, 128) for w in range(width)], axis=1)
+
+            def half(h, _):
+                rows = lhs[pl.ds(pl.multiple_of(256 * h, 256), 256), :]
+                acc = jnp.dot(rows, cols, preferred_element_type=F32)
                 for s in range(2):
                     for w in range(width):
                         part[2 * h + s, n + w] = acc[128 * s : 128 * (s + 1), 128 * w : 128 * (w + 1)].reshape(
                             NY, NCORE, 16, 128
                         )
-            n += width
+                return 0
+
+            for h in range(2):
+                half(h, 0)
+
+        def pair(i, _):
+            product(FIRST[j] + 2 * i, 2)
+            return 0
+
+        lax.fori_loop(0, PIECE[j] // 2, pair, 0)
+        if PIECE[j] % 2:
+            product(FIRST[j] + PIECE[j] - 1, 1)
         core_copy(j).start()
 
     def core_sum(j):
@@ -326,94 +335,100 @@
     hop(1, 0)
     hop(0, 0)
     fill()
+    mirror_send(4, 0)
+    mirror_send(4, 2)
+    x_first(0, 0)
+    forward(1, 0)
+    mirror_send(4, 3)
+    x_first(1, 0)
+    mirror_send(2, 3)
+    mirror_send(6, 1)
+    mirror_send(4, 1)
+    hop(0, 1)
+    hop(1, 1)
+    x_first(0, 1)
+    mirror_send(3, 2)
+    mirror_send(5, 2)
+    mirror_send(0, 1)
+    x_first(1, 1)
+    mirror_send(5, 3)
+    mirror_send(0, 2)
     mirror_send(5, 0)
-    mirror_send(4, 0)
-    mirror_send(1, 2)
-    mirror_send(4, 2)
+    mirror_send(3, 1)
+    mirror_send(0, 3)
+    hop(0, 2)
+    squares()
+    mirror_regroup(4)
     mirror_send(1, 0)
     mirror_send(1, 1)
+    mirror_send(6, 2)
+    mirror_send(1, 2)
+    mirror_send(3, 0)
+    mirror_send(2, 0)
+    x_first(0, 2)
+    mirror_send(1, 3)
+    mirror_send(6, 3)
+    mirror_regroup(0)
+    forward(0, 2)
+    hop(1, 2)
+    mirror_send(3, 3)
+    mirror_send(5, 1)
+    forward(1, 2)
+    hop(0, 3)
+    x_first(1, 2)
+    mirror_send(6, 0)
+    x_first(0, 3)
+    mirror_send(7, 0)
     mirror_send(7, 3)
-    x_first(0, 0)
-    mirror_send(7, 0)
-    mirror_send(4, 3)
-    mirror_send(3, 1)
-    mirror_send(6, 0)
-    hop(1, 1)
-    hop(0, 1)
-    x_first(1, 0)
-    mirror_send(0, 1)
-    mirror_send(0, 2)
-    squares()
-    mirror_send(4, 1)
-    x_first(1, 1)
-    mirror_send(3, 0)
-    x_first(0, 1)
-    forward(1, 1)
-    mirror_send(5, 2)
-    mirror_send(3, 3)
-    hop(1, 2)
-    mirror_send(6, 2)
-    forward(0, 0)
+    hop(1, 3)
     mirror_send(7, 1)
-    mirror_send(1, 3)
+    mirror_send(2, 2)
     mirror_send(7, 2)
-    hop(0, 2)
-    mirror_regroup(4)
-    x_first(1, 2)
-    mirror_send(0, 3)
-    mirror_send(6, 1)
-    mirror_send(2, 0)
-    mirror_send(3, 2)
-    hop(1, 3)
-    mirror_send(2, 2)
-    x_first(0, 2)
-    mirror_send(5, 1)
-    mirror_send(6, 3)
+    mirror_regroup(5)
     mirror_regroup(1)
-    x_first(1, 3)
-    forward(0, 2)
-    mirror_regroup(7)
-    mirror_send(5, 3)
-    sigma(4)
-    mirror_regroup(0)
     mirror_send(2, 1)
-    forward(1, 2)
-    mirror_send(2, 3)
+    hop(0, 4)
     mirror_regroup(3)
-    hop(0, 3)
-    x_first(0, 3)
-    forward(1, 0)
-    forward(1, 3)
-    sigma(3)
-    hop(1, 4)
-    x_first(1, 4)
     forward(0, 1)
     mirror_regroup(6)
+    forward(0, 3)
+    x_first(1, 3)
+    x_first(0, 4)
+    hop(1, 4)
+    forward(0, 0)
+    sigma(0)
     sigma(1)
+    forward(1, 3)
+    mirror_regroup(7)
     mirror_regroup(2)
-    sigma(0)
-    hop(0, 4)
-    x_first(0, 4)
-    mirror_regroup(5)
+    x_first(1, 4)
+    sigma(3)
+    forward(0, 4)
+    sigma(6)
+    forward(1, 1)
+    x_first(0, 5)
     forward(1, 4)
+    sigma(4)
     sigma(7)
+    sigma(5)
+    last(0)
     x_first(1, 5)
     sigma(2)
-    forward(0, 3)
-    sigma(6)
+    x_first(0, 6)
+    multiply(0)
+    multiply(1)
     last(1)
-    forward(0, 4)
-    x_first(0, 5)
     x_first(1, 6)
-    sigma(5)
-    multiply(1)
-    x_first(0, 6)
-    last(0)
-    multiply(0)
+    multiply(3)
+    core_sum(0)
+    multiply(2)
     core_sum(1)
-    core_sum(0)
+    core_sum(3)
+    core_sum(2)
+    y_sum(3)
+    y_sum(0)
     y_sum(1)
-    y_sum(0)
+    y_sum(2)
 
     for d in sent:
         d.wait_send()
@@ -429,6 +444,10 @@
 
 def body(g_hist, new_cols, row_time, drive_step, drive_levels):
     hbm = pl.BlockSpec(memory_space=pltpu.HBM)
+    operands = [
+        pltpu.with_memory_space_constraint(v, pltpu.HBM)
+        for v in (row_time, drive_step, drive_levels, g_hist, new_cols)
+    ]
     vmem = pl.BlockSpec(memory_space=pltpu.VMEM)
     dma = pltpu.SemaphoreType.DMA
     return pl.pallas_call(
@@ -441,14 +460,13 @@
             pltpu.SMEM((64,), jnp.int32),
             pltpu.VMEM((16, 128), F32),
             pltpu.VMEM((2, 2, 64, 16, 128), BF),
-            pltpu.VMEM((2, 2, 8, 16, 128), BF),
             pltpu.VMEM((NR, 2, 2, 2, 16, 128), BF),
             pltpu.VMEM((NR, 2, 2, 2, 16, 128), BF),
             pltpu.VMEM((NZ, NMODE, 2, 2, 16, 128), BF),
             pltpu.VMEM((NZ, NMODE, 2, 2, 16, 128), BF),
             pltpu.VMEM((NZ, 2, 2, 128, 128), F32),
             pltpu.VMEM((512, 2048), BF),
-            pltpu.VMEM((NZ, 2, NX, 32, 1024), BF),
+            pltpu.VMEM((NZ, 2, NX, 2, 8, 16, 128), BF),
             pltpu.VMEM((4, 8, NY, NCORE, 16, 128), F32),
             pltpu.VMEM((4, 8, NY, 16, 128), F32),
             pltpu.VMEM((4, 8, NY, 16, 128), YT),
@@ -460,10 +478,10 @@
             dma((len(PIECE),)), dma((len(PIECE),)), dma((len(PIECE), 3)), dma((len(PIECE), 3)),
         ],
         compiler_params=pltpu.CompilerParams(
-            collective_id=0, has_side_effects=True, vmem_limit_bytes=58 * 1024 * 1024
+            collective_id=0, has_side_effects=True, vmem_limit_bytes=40 * 1024 * 1024
         ),
         cost_estimate=pl.CostEstimate(flops=2147483648, bytes_accessed=1600000, transcendentals=0),
-    )(row_time, drive_step, drive_levels, g_hist, new_cols)
+    )(*operands)
 
 
 def solution(mesh):

time: 72.4 us -> 70 us (0.967)
  Pallas kernels: 70.6 us -> 69.2 us
  local copies, waits for them, and re-layouts: 1.67 us -> 0.71 us
    pallas_call x1, Pallas kernels: 70.6 us -> 69.2 us  [body(): pl.pallas_call(kernel, out_shape=jax.ShapeDtypeStruct((2, 2, 8, 16, 128),...]
    unnamed x1, local copies, waits for them, and re-layouts: 1.67 us -> 0.71 us
where the time goes in v3:
time: 70 us; the launch traced here: 69.9 us
  Pallas kernels  69.2 us (99%)
  local copies, waits for them, and re-layouts  0.71 us (1%)
    pallas_call x1, Pallas kernels, body(): pl.pallas_call(kernel, out_shape=jax.ShapeDtypeStruct((2, 2, 8, 16, 128),...  69.2 us

profile of v3, /device:TPU:1, one launch (start us, length us, event | category | flops | bytes accessed | tf_op | source)
XLA Modules:
  0.0 69.9 jit_solution(2640683697614895587)
XLA Ops:
  0.0 69.2 %shard_map.55 = f32[2,2,8,16,128]{4,3,2,1,0:T(8,128)S(1)} custom-call(s32[64]{0:T(128)} %rt_hbm.1, s32[64]{0:T(128)} %ds_hbm.1, f32[16,128]{1,0:T(8,128)} %dl_hbm.1, bf16[2,2,64,16,128]{4,3,2,1,0:T(8,128)(2,1)} %g_hbm.1, bf16[2,2,8,16,128]{4,3,2,1,0:T(8,128)(2,1)} %c_hbm.1), custom_call_target="tpu_custom_call" | custom-call | flops 2147483648 | bytes 1600000 | tf_op jit(solution)/shard_map/pallas_call | solution.py:453
  69.2 0.7 %copy.7 = f32[2,2,8,16,128]{4,3,2,1,0:T(8,128)} copy(f32[2,2,8,16,128]{4,3,2,1,0:T(8,128)S(1)} %shard_map.55) | data formatting | bytes 524288

commit v4 on v3

--- a/solution.py
+++ b/solution.py
@@ -10,9 +10,8 @@
 BF, F32 = jnp.bfloat16, jnp.float32
 MESH = pl.DeviceIdType.MESH
 
-CHUNK = ((3, 1), (3, 1))
-PIECE = (2, 2, 2, 2)
-YT = BF
+CHUNK = ((1, 1), (2, 0))
+PIECE = (2, 2)
 
 SCALE = 8.0 / 64
 
@@ -24,16 +23,18 @@
 
 A = [blocks(i, 0) for i in range(len(CHUNK))]
 B = [blocks(i, 1) for i in range(len(CHUNK))]
+LAST = 0
+SUM_ORDER = ((2, 0), (2, 1), (1, 0), (3, 0), (1, 1), (3, 1), (0, 1))
 FIRST = [sum(PIECE[:i]) for i in range(len(PIECE))]
 
 
 def kernel(
     rt_hbm, ds_hbm, dl_hbm, g_hbm, c_hbm, out,
     rt, ds, dl, g,
-    sb, rb, tb, mb, sq, lhs, rhs, part, cb, red, yb, kb,
+    sb, rb, tb, mb, sq, lhs, rhs, part, part16, gathered, kb,
     in_sem, s1_send, s1_recv, s2_send, s2_recv,
     za_s, za_r, xa_s, xa_r, xb_s, xb_r, zb_s, zb_r,
-    cx_s, cx_r, yx_s, yx_r,
+    sw_s, sw_r, sg_s, sg_r, sum_s, sum_r,
 ):
     r = lax.axis_index("trow")
     m = lax.axis_index("mode")
@@ -42,7 +43,7 @@
     loads = [
         pltpu.make_async_copy(src, dst, in_sem.at[i])
         for i, (src, dst) in enumerate(
-            ((g_hbm, g), (rt_hbm, rt), (c_hbm, rhs.at[z, :, x]), (ds_hbm, ds), (dl_hbm, dl))
+            ((g_hbm, g), (rt_hbm, rt), (c_hbm.at[:, :, pl.ds(4 * core, 4)], rhs.at[z, core, :, x]), (ds_hbm, ds), (dl_hbm, dl))
         )
     ]
     for load in loads:
@@ -71,7 +72,7 @@
     lax.fori_loop(0, NMODE - 1, greet_mode, 0)
 
     def fill():
-        for load in loads[:3]:
+        for load in loads[:2]:
             load.wait()
 
         def one(q, _):
@@ -87,16 +88,25 @@
 
     pl.semaphore_wait(bar, NR - 1 + NMODE - 1)
 
+    swap = pltpu.make_async_remote_copy(
+        c_hbm.at[:, :, pl.ds(4 * (1 - core), 4)], rhs.at[z, core, :, x], sw_s.at[0], sw_r.at[0],
+        device_id={"trow": r, "mode": y * NCORE + 1 - core}, device_id_type=MESH,
+    )
+    swap.start()
+
+    def swapped():
+        loads[2].wait()
+        swap.wait()
+
     sent = []
 
     def block(zz, xx, cols, half):
         h = slice(None) if half is None else half
-        return rhs.at[zz, h, slice(None) if xx is None else xx, :, pl.ds(*cols)]
-
-    def push(zz, xx, cols, half, ssem, rsem, dev, own=False):
-        dst = block(zz, xx, cols, half)
-        src = c_hbm.at[:, :, pl.ds(*cols)] if own else dst
-        d = pltpu.make_async_remote_copy(src, dst, ssem, rsem, device_id=dev, device_id_type=MESH)
+        return rhs.at[zz, :, h, slice(None) if xx is None else xx, :, pl.ds(*cols)]
+
+    def push(zz, xx, cols, half, ssem, rsem, dev):
+        ref = block(zz, xx, cols, half)
+        d = pltpu.make_async_remote_copy(ref, ref, ssem, rsem, device_id=dev, device_id_type=MESH)
         d.start()
         sent.append(d)
 
@@ -109,9 +119,8 @@
 
     def z_send(t, xx, cols, ssem, rsem):
         lo, hi = (None, None) if t < 4 else (0, 1)
-        own = t == 1 and xx is not None
-        push(at_z(-(t - 1)), xx, cols, lo, ssem.at[0, t - 1], rsem.at[0, t - 1], up, own)
-        push(at_z(t - 1), xx, cols, hi, ssem.at[1, t - 1], rsem.at[1, t - 1], down, own)
+        push(at_z(-(t - 1)), xx, cols, lo, ssem.at[0, t - 1], rsem.at[0, t - 1], up)
+        push(at_z(t - 1), xx, cols, hi, ssem.at[1, t - 1], rsem.at[1, t - 1], down)
 
     def z_wait(t, xx, cols, rsem):
         lo, hi = (None, None) if t < 4 else (0, 1)
@@ -119,8 +128,8 @@
         landed(at_z(t), xx, cols, hi, rsem.at[1, t - 1])
 
     def x_send(d, cols, ssem, rsem):
-        push(at_z(d), x, cols, None, ssem.at[0], rsem.at[0], right, d == 0)
-        push(at_z(d), x, cols, None, ssem.at[1], rsem.at[1], left, d == 0)
+        push(at_z(d), x, cols, None, ssem.at[0], rsem.at[0], right)
+        push(at_z(d), x, cols, None, ssem.at[1], rsem.at[1], left)
 
     def x_forward(d, cols, ssem, rsem):
         zz = at_z(d)
@@ -227,7 +236,7 @@
             return 0
 
         lax.fori_loop(0, NMODE - 1, arrive, 0)
-        base = pl.multiple_of(kg * 256, 256)
+        base = pl.multiple_of(kg * 512 + core * 256, 256)
         for s in range(2):
             hr = mb[kg, :, 0, s].reshape(128, 128).astype(F32)
             hi = mb[kg, :, 1, s].reshape(128, 128).astype(F32)
@@ -239,6 +248,20 @@
             lhs[pl.ds(128 * s, 128), hi_lanes] = (-si).astype(BF)
             lhs[pl.ds(256 + 128 * s, 128), lo] = si.astype(BF)
             lhs[pl.ds(256 + 128 * s, 128), hi_lanes] = sr.astype(BF)
+
+        sigma_copy(d).start()
+
+    def sigma_copy(d):
+        here = lhs.at[:, pl.ds(pl.multiple_of(at_z(-d) * 512 + core * 256, 256), 256)]
+        return pltpu.make_async_remote_copy(
+            here, here, sg_s.at[d], sg_r.at[d],
+            device_id={"trow": r, "mode": y * NCORE + 1 - core}, device_id_type=MESH,
+        )
+
+    def sigmas_landed():
+        for d in range(NZ):
+            other = lhs.at[:, pl.ds(pl.multiple_of(at_z(-d) * 512 + (1 - core) * 256, 256), 256)]
+            pltpu.make_async_copy(other, other, sg_r.at[d]).wait()
 
     def squares():
         loads[3].wait()
@@ -276,170 +299,149 @@
 
         lax.fori_loop(0, NZ, one, 0)
 
-    def core_copy(j):
+    def sum_copy(j, e, other):
         here = pl.ds(FIRST[j], PIECE[j])
+        ty, tc = (y + e) % NY, (1 - core if other else core)
         return pltpu.make_async_remote_copy(
-            part.at[:, here, :, 1 - core], cb.at[:, here], cx_s.at[j], cx_r.at[j],
-            device_id={"trow": r, "mode": y * NCORE + 1 - core}, device_id_type=MESH,
-        )
-
-    def y_copy(j, e):
-        here = pl.ds(FIRST[j], PIECE[j])
-        to = (y + e) % NY
-        return pltpu.make_async_remote_copy(
-            red.at[:, here, to], yb.at[e - 1, :, here], yx_s.at[j, e - 1], yx_r.at[j, e - 1],
-            device_id={"trow": r, "mode": to * NCORE + core}, device_id_type=MESH,
+            part16.at[:, here, ty, tc], gathered.at[other, e, :, here], sum_s.at[j, other, e], sum_r.at[j, other, e],
+            device_id={"trow": r, "mode": ty * NCORE + tc}, device_id_type=MESH,
         )
 
     def multiply(j):
         def product(n, width):
-            cols = jnp.concatenate([rhs[:, :, :, :, n + w].reshape(2048, 128) for w in range(width)], axis=1)
-
-            def half(h, _):
-                rows = lhs[pl.ds(pl.multiple_of(256 * h, 256), 256), :]
+            cols = jnp.concatenate([rhs[:, :, :, :, :, n + w].reshape(4096, 128) for w in range(width)], axis=1)
+            for h in range(2):
+                rows = lhs[256 * h : 256 * (h + 1), :]
                 acc = jnp.dot(rows, cols, preferred_element_type=F32)
                 for s in range(2):
                     for w in range(width):
-                        part[2 * h + s, n + w] = acc[128 * s : 128 * (s + 1), 128 * w : 128 * (w + 1)].reshape(
-                            NY, NCORE, 16, 128
-                        )
-                return 0
-
-            for h in range(2):
-                half(h, 0)
-
-        def pair(i, _):
+                        tile = acc[128 * s : 128 * (s + 1), 128 * w : 128 * (w + 1)].reshape(NY, NCORE, 16, 128)
+                        part[2 * h + s, n + w] = tile
+                        part16[2 * h + s, n + w] = tile.astype(BF)
+
+        for i in range(PIECE[j] // 2):
             product(FIRST[j] + 2 * i, 2)
-            return 0
-
-        lax.fori_loop(0, PIECE[j] // 2, pair, 0)
         if PIECE[j] % 2:
             product(FIRST[j] + PIECE[j] - 1, 1)
-        core_copy(j).start()
-
-    def core_sum(j):
-        core_copy(j).wait_recv()
+        for e, other in SUM_ORDER:
+            sum_copy(j, e, other).start()
+
+    def y_sum(j):
+        for e, other in SUM_ORDER:
+            sum_copy(j, e, other).wait_recv()
         here = pl.ds(FIRST[j], PIECE[j])
-        red[:, here] = (part[:, here, :, core] + cb[:, here]).astype(YT)
-        for e in (2, 1, 3):
-            y_copy(j, e).start()
-
-    def y_sum(j):
-        for e in (2, 1, 3):
-            y_copy(j, e).wait_recv()
-        here = pl.ds(FIRST[j], PIECE[j])
-        own = part[:, here, y, core] + cb[:, here, y]
-        total = own + (yb[1, :, here].astype(F32) + (yb[0, :, here].astype(F32) + yb[2, :, here].astype(F32)))
-        out[:, :, here] = (total * SCALE).reshape(2, 2, PIECE[j], 16, 128)
-
+        mine = part[:, here, y, core]
+        theirs = gathered[1, 0, :, here].astype(F32)
+        for e in range(1, NY):
+            mine += gathered[0, e, :, here].astype(F32)
+            theirs += gathered[1, e, :, here].astype(F32)
+        out[:, :, pl.ds(4 * core + FIRST[j], PIECE[j])] = (mine * SCALE).reshape(2, 2, PIECE[j], 16, 128)
+        out[:, :, pl.ds(4 * (1 - core) + FIRST[j], PIECE[j])] = (theirs * SCALE).reshape(2, 2, PIECE[j], 16, 128)
+
+    def sums_left(j):
+        for e, other in SUM_ORDER:
+            sum_copy(j, e, other).wait_send()
+
+    def drain():
+        for d in sent:
+            d.wait_send()
+        all_but_one = sb.at[pl.ds(0, NR - 1)]
+        pltpu.make_async_copy(all_but_one, all_but_one, s1_send.at[0]).wait()
+        all_but_own = tb.at[:, pl.ds(0, NMODE - 1)]
+        pltpu.make_async_copy(all_but_own, all_but_own, s2_send.at[0]).wait()
+        for d in range(NZ):
+            sigma_copy(d).wait_send()
+        for j in range(len(PIECE)):
+            if j != LAST:
+                sums_left(j)
+
+    fill()
+    mirror_send(2, 0)
+    mirror_send(7, 0)
+    mirror_send(4, 1)
+    mirror_send(6, 0)
+    mirror_send(1, 0)
+    mirror_send(2, 1)
+    mirror_send(5, 2)
+    mirror_send(7, 2)
+    squares()
+    mirror_send(6, 2)
+    mirror_send(3, 2)
+    mirror_send(7, 1)
+    swapped()
+    mirror_send(7, 3)
+    hop(0, 0)
+    mirror_send(6, 1)
+    mirror_send(0, 3)
     hop(1, 0)
-    hop(0, 0)
-    fill()
-    mirror_send(4, 0)
-    mirror_send(4, 2)
+    mirror_send(6, 3)
+    mirror_send(3, 3)
+    mirror_send(2, 3)
     x_first(0, 0)
+    mirror_send(3, 0)
+    mirror_send(5, 0)
+    mirror_send(2, 2)
+    mirror_send(0, 2)
     forward(1, 0)
-    mirror_send(4, 3)
-    x_first(1, 0)
-    mirror_send(2, 3)
-    mirror_send(6, 1)
-    mirror_send(4, 1)
+    mirror_send(1, 2)
     hop(0, 1)
+    mirror_send(0, 1)
+    x_first(0, 1)
     hop(1, 1)
-    x_first(0, 1)
-    mirror_send(3, 2)
-    mirror_send(5, 2)
-    mirror_send(0, 1)
-    x_first(1, 1)
+    mirror_regroup(0)
+    x_first(0, 2)
+    mirror_regroup(6)
+    forward(0, 1)
     mirror_send(5, 3)
-    mirror_send(0, 2)
-    mirror_send(5, 0)
+    mirror_send(1, 3)
     mirror_send(3, 1)
-    mirror_send(0, 3)
-    hop(0, 2)
-    squares()
-    mirror_regroup(4)
-    mirror_send(1, 0)
-    mirror_send(1, 1)
-    mirror_send(6, 2)
-    mirror_send(1, 2)
-    mirror_send(3, 0)
-    mirror_send(2, 0)
-    x_first(0, 2)
-    mirror_send(1, 3)
-    mirror_send(6, 3)
-    mirror_regroup(0)
-    forward(0, 2)
     hop(1, 2)
-    mirror_send(3, 3)
     mirror_send(5, 1)
-    forward(1, 2)
-    hop(0, 3)
-    x_first(1, 2)
-    mirror_send(6, 0)
-    x_first(0, 3)
-    mirror_send(7, 0)
-    mirror_send(7, 3)
-    hop(1, 3)
-    mirror_send(7, 1)
-    mirror_send(2, 2)
-    mirror_send(7, 2)
-    mirror_regroup(5)
-    mirror_regroup(1)
-    mirror_send(2, 1)
-    hop(0, 4)
-    mirror_regroup(3)
-    forward(0, 1)
-    mirror_regroup(6)
-    forward(0, 3)
-    x_first(1, 3)
-    x_first(0, 4)
-    hop(1, 4)
-    forward(0, 0)
-    sigma(0)
-    sigma(1)
-    forward(1, 3)
     mirror_regroup(7)
     mirror_regroup(2)
-    x_first(1, 4)
+    mirror_send(1, 1)
+    sigma(6)
+    mirror_send(4, 2)
+    mirror_send(4, 3)
+    mirror_send(4, 0)
+    hop(0, 2)
+    mirror_regroup(3)
+    sigma(7)
+    sigma(0)
+    hop(1, 3)
+    mirror_regroup(1)
+    forward(0, 2)
+    mirror_regroup(5)
     sigma(3)
+    forward(1, 2)
+    x_first(0, 3)
+    forward(1, 1)
+    mirror_regroup(4)
+    hop(1, 4)
+    sigma(5)
+    hop(0, 3)
+    x_first(0, 4)
+    hop(0, 4)
+    sigma(4)
+    forward(1, 4)
+    forward(1, 3)
+    sigma(2)
+    forward(0, 0)
+    sigma(1)
+    forward(0, 3)
+    x_first(0, 5)
     forward(0, 4)
-    sigma(6)
-    forward(1, 1)
-    x_first(0, 5)
-    forward(1, 4)
-    sigma(4)
-    sigma(7)
-    sigma(5)
+    sigmas_landed()
+    last(1)
+    multiply(1)
     last(0)
-    x_first(1, 5)
-    sigma(2)
     x_first(0, 6)
     multiply(0)
-    multiply(1)
-    last(1)
-    x_first(1, 6)
-    multiply(3)
-    core_sum(0)
-    multiply(2)
-    core_sum(1)
-    core_sum(3)
-    core_sum(2)
-    y_sum(3)
+    y_sum(1)
+    drain()
     y_sum(0)
-    y_sum(1)
-    y_sum(2)
-
-    for d in sent:
-        d.wait_send()
-    all_but_one = sb.at[pl.ds(0, NR - 1)]
-    pltpu.make_async_copy(all_but_one, all_but_one, s1_send.at[0]).wait()
-    all_but_own = tb.at[:, pl.ds(0, NMODE - 1)]
-    pltpu.make_async_copy(all_but_own, all_but_own, s2_send.at[0]).wait()
-    for j in range(len(PIECE)):
-        core_copy(j).wait_send()
-        for e in (2, 1, 3):
-            y_copy(j, e).wait_send()
+
+    sums_left(LAST)
 
 
 def body(g_hist, new_cols, row_time, drive_step, drive_levels):
@@ -465,17 +467,16 @@
             pltpu.VMEM((NZ, NMODE, 2, 2, 16, 128), BF),
             pltpu.VMEM((NZ, NMODE, 2, 2, 16, 128), BF),
             pltpu.VMEM((NZ, 2, 2, 128, 128), F32),
-            pltpu.VMEM((512, 2048), BF),
-            pltpu.VMEM((NZ, 2, NX, 2, 8, 16, 128), BF),
-            pltpu.VMEM((4, 8, NY, NCORE, 16, 128), F32),
-            pltpu.VMEM((4, 8, NY, 16, 128), F32),
-            pltpu.VMEM((4, 8, NY, 16, 128), YT),
-            pltpu.VMEM((3, 4, 8, 16, 128), YT),
+            pltpu.VMEM((512, 4096), BF),
+            pltpu.VMEM((NZ, NCORE, 2, NX, 2, 4, 16, 128), BF),
+            pltpu.VMEM((4, 4, NY, NCORE, 16, 128), F32),
+            pltpu.VMEM((4, 4, NY, NCORE, 16, 128), BF),
+            pltpu.VMEM((2, NY, 4, 4, 16, 128), BF),
             pltpu.VMEM((2, 9, 8, 128), F32),
             dma((5,)), dma((1,)), dma((NR,)), dma((1,)), dma((NZ, NMODE)),
             dma((len(CHUNK), 2, 4)), dma((len(CHUNK), 2, 4)), dma((len(CHUNK), NZ, 4)), dma((len(CHUNK), NZ, 4)),
             dma((len(CHUNK), 4)), dma((len(CHUNK), 4)), dma((len(CHUNK), 2, 4)), dma((len(CHUNK), 2, 4)),
-            dma((len(PIECE),)), dma((len(PIECE),)), dma((len(PIECE), 3)), dma((len(PIECE), 3)),
+            dma((1,)), dma((1,)), dma((NZ,)), dma((NZ,)), dma((len(PIECE), 2, NY)), dma((len(PIECE), 2, NY)),
         ],
         compiler_params=pltpu.CompilerParams(
             collective_id=0, has_side_effects=True, vmem_limit_bytes=40 * 1024 * 1024

time: 70 us -> 69.3 us (0.990)
  Pallas kernels: 69.2 us -> 68.5 us
    pallas_call x1, Pallas kernels: 69.2 us -> 68.5 us  [body(): pl.pallas_call(kernel, out_shape=jax.ShapeDtypeStruct((2, 2, 8, 16, 128),...]
where the time goes in v4:
time: 69.3 us; the launch traced here: 69.2 us
  Pallas kernels  68.5 us (99%)
  local copies, waits for them, and re-layouts  0.71 us (1%)
    pallas_call x1, Pallas kernels, body(): pl.pallas_call(kernel, out_shape=jax.ShapeDtypeStruct((2, 2, 8, 16, 128),...  68.5 us

profile of v4, /device:TPU:1, one launch (start us, length us, event | category | flops | bytes accessed | tf_op | source)
XLA Modules:
  0.0 69.2 jit_solution(4537430515354608815)
XLA Ops:
  0.0 68.5 %shard_map.55 = f32[2,2,8,16,128]{4,3,2,1,0:T(8,128)S(1)} custom-call(s32[64]{0:T(128)} %rt_hbm.1, s32[64]{0:T(128)} %ds_hbm.1, f32[16,128]{1,0:T(8,128)} %dl_hbm.1, bf16[2,2,64,16,128]{4,3,2,1,0:T(8,128)(2,1)} %g_hbm.1, bf16[2,2,8,16,128]{4,3,2,1,0:T(8,128)(2,1)} %c_hbm.1), custom_call_target="tpu_custom_call" | custom-call | flops 2147483648 | bytes 1600000 | tf_op jit(solution)/shard_map/pallas_call | solution.py:455
  68.5 0.7 %copy.7 = f32[2,2,8,16,128]{4,3,2,1,0:T(8,128)} copy(f32[2,2,8,16,128]{4,3,2,1,0:T(8,128)S(1)} %shard_map.55) | data formatting | bytes 524288

commit v5 on v4

--- a/solution.py
+++ b/solution.py
@@ -10,7 +10,7 @@
 BF, F32 = jnp.bfloat16, jnp.float32
 MESH = pl.DeviceIdType.MESH
 
-CHUNK = ((1, 1), (2, 0))
+CHUNK = ((4, 0), (3, 1))
 PIECE = (2, 2)
 
 SCALE = 8.0 / 64
@@ -23,7 +23,8 @@
 
 A = [blocks(i, 0) for i in range(len(CHUNK))]
 B = [blocks(i, 1) for i in range(len(CHUNK))]
-LAST = 0
+LAST = 1
+FAR = ((0, 1, 2, 6, 7), (3, 4, 5))
 SUM_ORDER = ((2, 0), (2, 1), (1, 0), (3, 0), (1, 1), (3, 1), (0, 1))
 FIRST = [sum(PIECE[:i]) for i in range(len(PIECE))]
 
@@ -32,7 +33,7 @@
     rt_hbm, ds_hbm, dl_hbm, g_hbm, c_hbm, out,
     rt, ds, dl, g,
     sb, rb, tb, mb, sq, lhs, rhs, part, part16, gathered, kb,
-    in_sem, s1_send, s1_recv, s2_send, s2_recv,
+    in_sem, col_sem, s1_send, s1_recv, s2_send, s2_recv,
     za_s, za_r, xa_s, xa_r, xb_s, xb_r, zb_s, zb_r,
     sw_s, sw_r, sg_s, sg_r, sum_s, sum_r,
 ):
@@ -43,10 +44,16 @@
     loads = [
         pltpu.make_async_copy(src, dst, in_sem.at[i])
         for i, (src, dst) in enumerate(
-            ((g_hbm, g), (rt_hbm, rt), (c_hbm.at[:, :, pl.ds(4 * core, 4)], rhs.at[z, core, :, x]), (ds_hbm, ds), (dl_hbm, dl))
+            ((g_hbm, g), (rt_hbm, rt), (ds_hbm, ds), (dl_hbm, dl))
         )
     ]
-    for load in loads:
+    own_cols = [
+        pltpu.make_async_copy(
+            c_hbm.at[:, i % 2, 4 * core + i // 2], rhs.at[z, core, :, x, i], col_sem.at[i]
+        )
+        for i in range(8)
+    ]
+    for load in loads + own_cols:
         load.start()
 
     def at_z(d):
@@ -88,21 +95,25 @@
 
     pl.semaphore_wait(bar, NR - 1 + NMODE - 1)
 
-    swap = pltpu.make_async_remote_copy(
-        c_hbm.at[:, :, pl.ds(4 * (1 - core), 4)], rhs.at[z, core, :, x], sw_s.at[0], sw_r.at[0],
-        device_id={"trow": r, "mode": y * NCORE + 1 - core}, device_id_type=MESH,
-    )
-    swap.start()
+    swaps = [
+        pltpu.make_async_remote_copy(
+            c_hbm.at[:, i % 2, 4 * (1 - core) + i // 2], rhs.at[z, core, :, x, i], sw_s.at[i], sw_r.at[i],
+            device_id={"trow": r, "mode": y * NCORE + 1 - core}, device_id_type=MESH,
+        )
+        for i in range(8)
+    ]
+    for swap in swaps:
+        swap.start()
 
     def swapped():
-        loads[2].wait()
-        swap.wait()
+        for copy in own_cols + swaps:
+            copy.wait()
 
     sent = []
 
     def block(zz, xx, cols, half):
         h = slice(None) if half is None else half
-        return rhs.at[zz, :, h, slice(None) if xx is None else xx, :, pl.ds(*cols)]
+        return rhs.at[zz, :, h, slice(None) if xx is None else xx, pl.ds(*cols)]
 
     def push(zz, xx, cols, half, ssem, rsem, dev):
         ref = block(zz, xx, cols, half)
@@ -161,8 +172,8 @@
         for d in {0: (0,), 4: (4,)}.get(t, (-t, t)):
             x_forward(d, A[ch], *xa(ch, d))
 
-    def last(ch):
-        for d in range(NZ):
+    def last(ch, far):
+        for d in FAR[far]:
             x_last(d, A[ch], xa(ch, d)[1])
 
     def x_first(ch, t):
@@ -258,14 +269,14 @@
             device_id={"trow": r, "mode": y * NCORE + 1 - core}, device_id_type=MESH,
         )
 
-    def sigmas_landed():
-        for d in range(NZ):
+    def sigmas_landed(far):
+        for d in FAR[far]:
             other = lhs.at[:, pl.ds(pl.multiple_of(at_z(-d) * 512 + (1 - core) * 256, 256), 256)]
             pltpu.make_async_copy(other, other, sg_r.at[d]).wait()
 
     def squares():
+        loads[2].wait()
         loads[3].wait()
-        loads[4].wait()
 
         def strengths(k, _):
             t = rt[k]
@@ -309,7 +320,7 @@
 
     def multiply(j):
         def product(n, width):
-            cols = jnp.concatenate([rhs[:, :, :, :, :, n + w].reshape(4096, 128) for w in range(width)], axis=1)
+            cols = jnp.concatenate([rhs[:, :, :, :, 2 * (n + w) : 2 * (n + w) + 2].reshape(4096, 128) for w in range(width)], axis=1)
             for h in range(2):
                 rows = lhs[256 * h : 256 * (h + 1), :]
                 acc = jnp.dot(rows, cols, preferred_element_type=F32)
@@ -356,90 +367,93 @@
                 sums_left(j)
 
     fill()
+    mirror_send(5, 0)
+    mirror_send(7, 2)
     mirror_send(2, 0)
-    mirror_send(7, 0)
-    mirror_send(4, 1)
-    mirror_send(6, 0)
+    mirror_send(2, 3)
+    mirror_send(0, 1)
+    mirror_send(6, 3)
     mirror_send(1, 0)
-    mirror_send(2, 1)
-    mirror_send(5, 2)
-    mirror_send(7, 2)
-    squares()
-    mirror_send(6, 2)
-    mirror_send(3, 2)
-    mirror_send(7, 1)
     swapped()
     mirror_send(7, 3)
     hop(0, 0)
+    mirror_send(5, 1)
+    mirror_send(2, 2)
+    mirror_send(3, 1)
+    mirror_send(1, 1)
+    mirror_send(3, 0)
+    mirror_send(0, 2)
     mirror_send(6, 1)
     mirror_send(0, 3)
+    x_first(1, 0)
     hop(1, 0)
-    mirror_send(6, 3)
+    mirror_send(5, 2)
+    hop(0, 1)
+    mirror_send(7, 1)
+    mirror_send(3, 2)
+    mirror_send(1, 2)
     mirror_send(3, 3)
-    mirror_send(2, 3)
-    x_first(0, 0)
-    mirror_send(3, 0)
-    mirror_send(5, 0)
-    mirror_send(2, 2)
-    mirror_send(0, 2)
+    x_first(1, 1)
+    mirror_regroup(0)
+    forward(0, 0)
+    mirror_send(6, 0)
+    mirror_send(1, 3)
+    squares()
+    mirror_send(5, 3)
+    mirror_send(4, 1)
+    mirror_send(6, 2)
+    forward(0, 1)
+    mirror_send(7, 0)
+    hop(0, 2)
+    hop(1, 1)
+    mirror_send(2, 1)
+    mirror_send(4, 2)
+    mirror_regroup(5)
+    mirror_send(4, 3)
     forward(1, 0)
-    mirror_send(1, 2)
-    hop(0, 1)
-    mirror_send(0, 1)
-    x_first(0, 1)
-    hop(1, 1)
-    mirror_regroup(0)
-    x_first(0, 2)
+    mirror_regroup(3)
+    x_first(1, 2)
+    forward(0, 2)
     mirror_regroup(6)
-    forward(0, 1)
-    mirror_send(5, 3)
-    mirror_send(1, 3)
-    mirror_send(3, 1)
-    hop(1, 2)
-    mirror_send(5, 1)
-    mirror_regroup(7)
-    mirror_regroup(2)
-    mirror_send(1, 1)
-    sigma(6)
-    mirror_send(4, 2)
-    mirror_send(4, 3)
-    mirror_send(4, 0)
-    hop(0, 2)
-    mirror_regroup(3)
-    sigma(7)
-    sigma(0)
-    hop(1, 3)
     mirror_regroup(1)
-    forward(0, 2)
-    mirror_regroup(5)
-    sigma(3)
-    forward(1, 2)
-    x_first(0, 3)
-    forward(1, 1)
-    mirror_regroup(4)
-    hop(1, 4)
     sigma(5)
     hop(0, 3)
-    x_first(0, 4)
+    mirror_send(4, 0)
+    hop(1, 2)
+    mirror_regroup(7)
+    sigma(6)
+    mirror_regroup(2)
+    forward(0, 3)
+    x_first(1, 3)
+    sigma(1)
     hop(0, 4)
+    mirror_regroup(4)
+    hop(1, 3)
+    sigma(0)
+    x_first(1, 4)
+    forward(0, 4)
+    sigma(3)
+    sigma(2)
+    hop(1, 4)
+    forward(1, 1)
     sigma(4)
+    sigma(7)
+    forward(1, 3)
+    x_first(1, 5)
+    last(0, 1)
+    forward(1, 2)
+    last(0, 0)
     forward(1, 4)
-    forward(1, 3)
-    sigma(2)
-    forward(0, 0)
-    sigma(1)
-    forward(0, 3)
-    x_first(0, 5)
-    forward(0, 4)
-    sigmas_landed()
-    last(1)
+    sigmas_landed(1)
+    sigmas_landed(0)
+    multiply(0)
+    last(1, 0)
+    x_first(1, 6)
+    last(1, 1)
     multiply(1)
-    last(0)
-    x_first(0, 6)
-    multiply(0)
+    y_sum(0)
+    drain()
     y_sum(1)
-    drain()
-    y_sum(0)
 
     sums_left(LAST)
 
@@ -468,15 +482,15 @@
             pltpu.VMEM((NZ, NMODE, 2, 2, 16, 128), BF),
             pltpu.VMEM((NZ, 2, 2, 128, 128), F32),
             pltpu.VMEM((512, 4096), BF),
-            pltpu.VMEM((NZ, NCORE, 2, NX, 2, 4, 16, 128), BF),
+            pltpu.VMEM((NZ, NCORE, 2, NX, 8, 16, 128), BF),
             pltpu.VMEM((4, 4, NY, NCORE, 16, 128), F32),
             pltpu.VMEM((4, 4, NY, NCORE, 16, 128), BF),
             pltpu.VMEM((2, NY, 4, 4, 16, 128), BF),
             pltpu.VMEM((2, 9, 8, 128), F32),
-            dma((5,)), dma((1,)), dma((NR,)), dma((1,)), dma((NZ, NMODE)),
+            dma((4,)), dma((8,)), dma((1,)), dma((NR,)), dma((1,)), dma((NZ, NMODE)),
             dma((len(CHUNK), 2, 4)), dma((len(CHUNK), 2, 4)), dma((len(CHUNK), NZ, 4)), dma((len(CHUNK), NZ, 4)),
             dma((len(CHUNK), 4)), dma((len(CHUNK), 4)), dma((len(CHUNK), 2, 4)), dma((len(CHUNK), 2, 4)),
-            dma((1,)), dma((1,)), dma((NZ,)), dma((NZ,)), dma((len(PIECE), 2, NY)), dma((len(PIECE), 2, NY)),
+            dma((8,)), dma((8,)), dma((NZ,)), dma((NZ,)), dma((len(PIECE), 2, NY)), dma((len(PIECE), 2, NY)),
         ],
         compiler_params=pltpu.CompilerParams(
             collective_id=0, has_side_effects=True, vmem_limit_bytes=40 * 1024 * 1024

time: 69.3 us -> 68.4 us (0.987)
  Pallas kernels: 68.5 us -> 67.6 us
    pallas_call x1, Pallas kernels: 68.5 us -> 67.6 us  [body(): pl.pallas_call(kernel, out_shape=jax.ShapeDtypeStruct((2, 2, 8, 16, 128),...]
where the time goes in v5:
time: 68.4 us; the launch traced here: 68.3 us
  Pallas kernels  67.6 us (99%)
  local copies, waits for them, and re-layouts  0.71 us (1%)
    pallas_call x1, Pallas kernels, body(): pl.pallas_call(kernel, out_shape=jax.ShapeDtypeStruct((2, 2, 8, 16, 128),...  67.6 us

profile of v5, /device:TPU:1, one launch (start us, length us, event | category | flops | bytes accessed | tf_op | source)
XLA Modules:
  0.0 68.3 jit_solution(3933398088059385836)
XLA Ops:
  0.0 67.6 %shard_map.55 = f32[2,2,8,16,128]{4,3,2,1,0:T(8,128)S(1)} custom-call(s32[64]{0:T(128)} %rt_hbm.1, s32[64]{0:T(128)} %ds_hbm.1, f32[16,128]{1,0:T(8,128)} %dl_hbm.1, bf16[2,2,64,16,128]{4,3,2,1,0:T(8,128)(2,1)} %g_hbm.1, bf16[2,2,8,16,128]{4,3,2,1,0:T(8,128)(2,1)} %c_hbm.1), custom_call_target="tpu_custom_call" | custom-call | flops 2147483648 | bytes 1600000 | tf_op jit(solution)/shard_map/pallas_call | solution.py:469
  67.6 0.7 %copy.7 = f32[2,2,8,16,128]{4,3,2,1,0:T(8,128)} copy(f32[2,2,8,16,128]{4,3,2,1,0:T(8,128)S(1)} %shard_map.55) | data formatting | bytes 524288

commit v6 on v5

--- a/solution.py
+++ b/solution.py
@@ -31,11 +31,11 @@
 
 def kernel(
     rt_hbm, ds_hbm, dl_hbm, g_hbm, c_hbm, out,
-    rt, ds, dl, g,
+    rt, ds, dl, g, give,
     sb, rb, tb, mb, sq, lhs, rhs, part, part16, gathered, kb,
     in_sem, col_sem, s1_send, s1_recv, s2_send, s2_recv,
     za_s, za_r, xa_s, xa_r, xb_s, xb_r, zb_s, zb_r,
-    sw_s, sw_r, sg_s, sg_r, sum_s, sum_r,
+    own_s, sw_s, sw_r, sg_s, sg_r, sum_s, sum_r,
 ):
     r = lax.axis_index("trow")
     m = lax.axis_index("mode")
@@ -53,7 +53,13 @@
         )
         for i in range(8)
     ]
-    for load in loads + own_cols:
+    give_cols = [
+        pltpu.make_async_copy(
+            c_hbm.at[:, i % 2, 4 * (1 - core) + i // 2], give.at[:, i], col_sem.at[8 + i]
+        )
+        for i in range(8)
+    ]
+    for load in own_cols + give_cols + loads:
         load.start()
 
     def at_z(d):
@@ -62,8 +68,11 @@
     def at_x(d):
         return (x + d + NX) % NX
 
-    def trow_dev(zz, xx):
-        return {"trow": zz * NX + xx, "mode": m}
+    def row_of(zz, xx):
+        return zz * NX + xx
+
+    up_row, down_row = row_of(at_z(1), x), row_of(at_z(-1), x)
+    right_row, left_row = row_of(z, at_x(1)), row_of(z, at_x(-1))
 
     bar = pltpu.get_barrier_semaphore()
 
@@ -77,6 +86,11 @@
 
     lax.fori_loop(0, NR - 1, greet_trow, 0)
     lax.fori_loop(0, NMODE - 1, greet_mode, 0)
+    crossing = [{"trow": q, "mode": y * NCORE + 1 - core} for q in (up_row, down_row, right_row, left_row)]
+    for dev in crossing:
+        pl.semaphore_signal(bar, inc=1, device_id=dev, device_id_type=MESH)
+    for copy in own_cols + give_cols:
+        copy.wait()
 
     def fill():
         for load in loads[:2]:
@@ -93,21 +107,16 @@
         lax.fori_loop(0, NR, one, 0)
         rb[r] = sb[r]
 
-    pl.semaphore_wait(bar, NR - 1 + NMODE - 1)
-
-    swaps = [
-        pltpu.make_async_remote_copy(
-            c_hbm.at[:, i % 2, 4 * (1 - core) + i // 2], rhs.at[z, core, :, x, i], sw_s.at[i], sw_r.at[i],
-            device_id={"trow": r, "mode": y * NCORE + 1 - core}, device_id_type=MESH,
-        )
-        for i in range(8)
-    ]
-    for swap in swaps:
-        swap.start()
+    pl.semaphore_wait(bar, NR - 1 + NMODE - 1 + 4)
+
+    swap = pltpu.make_async_remote_copy(
+        give, rhs.at[z, core, :, x], sw_s.at[0], sw_r.at[0],
+        device_id={"trow": r, "mode": y * NCORE + 1 - core}, device_id_type=MESH,
+    )
+    swap.start()
 
     def swapped():
-        for copy in own_cols + swaps:
-            copy.wait()
+        swap.wait()
 
     sent = []
 
@@ -125,10 +134,22 @@
         ref = block(zz, xx, cols, half)
         pltpu.make_async_copy(ref, ref, rsem).wait()
 
-    up, down = trow_dev(at_z(1), x), trow_dev(at_z(-1), x)
-    right, left = trow_dev(z, at_x(1)), trow_dev(z, at_x(-1))
-
-    def z_send(t, xx, cols, ssem, rsem):
+    def push_own(cols, way, ssem, osem, rsem):
+        row = (up_row, down_row, right_row, left_row)[way]
+        dst = rhs.at[z, core, :, x, pl.ds(*cols)]
+        for src, sem, dev in ((dst, ssem, {"trow": row, "mode": m}), (give.at[:, pl.ds(*cols)], osem, crossing[way])):
+            d = pltpu.make_async_remote_copy(src, dst, sem, rsem, device_id=dev, device_id_type=MESH)
+            d.start()
+            sent.append(d)
+
+    up, down = {"trow": up_row, "mode": m}, {"trow": down_row, "mode": m}
+    right, left = {"trow": right_row, "mode": m}, {"trow": left_row, "mode": m}
+
+    def z_send(t, xx, cols, ssem, rsem, osem=None):
+        if osem is not None and t == 1:
+            push_own(cols, 0, ssem.at[0, 0], osem.at[0], rsem.at[0, 0])
+            push_own(cols, 1, ssem.at[1, 0], osem.at[1], rsem.at[1, 0])
+            return
         lo, hi = (None, None) if t < 4 else (0, 1)
         push(at_z(-(t - 1)), xx, cols, lo, ssem.at[0, t - 1], rsem.at[0, t - 1], up)
         push(at_z(t - 1), xx, cols, hi, ssem.at[1, t - 1], rsem.at[1, t - 1], down)
@@ -138,7 +159,11 @@
         landed(at_z(-t), xx, cols, lo, rsem.at[0, t - 1])
         landed(at_z(t), xx, cols, hi, rsem.at[1, t - 1])
 
-    def x_send(d, cols, ssem, rsem):
+    def x_send(d, cols, ssem, rsem, osem):
+        if d == 0:
+            push_own(cols, 2, ssem.at[0], osem.at[0], rsem.at[0])
+            push_own(cols, 3, ssem.at[1], osem.at[1], rsem.at[1])
+            return
         push(at_z(d), x, cols, None, ssem.at[0], rsem.at[0], right)
         push(at_z(d), x, cols, None, ssem.at[1], rsem.at[1], left)
 
@@ -164,9 +189,9 @@
         if t > 0:
             z_wait(t, x, A[ch], za(ch)[1])
         if t < 4:
-            z_send(t + 1, x, A[ch], *za(ch))
+            z_send(t + 1, x, A[ch], *za(ch), own_s.at[ch, 0])
         for d in {0: (0,), 4: (4,)}.get(t, (-t, t)):
-            x_send(d, A[ch], *xa(ch, d))
+            x_send(d, A[ch], *xa(ch, d), own_s.at[ch, 1])
 
     def forward(ch, t):
         for d in {0: (0,), 4: (4,)}.get(t, (-t, t)):
@@ -180,7 +205,7 @@
         xb = (xb_s.at[ch], xb_r.at[ch])
         zb = (zb_s.at[ch], zb_r.at[ch])
         if t == 0:
-            x_send(0, B[ch], *xb)
+            x_send(0, B[ch], *xb, own_s.at[ch, 2])
         if t == 1:
             x_forward(0, B[ch], *xb)
         if t == 2:
@@ -366,86 +391,86 @@
             if j != LAST:
                 sums_left(j)
 
+    hop(0, 0)
     fill()
+    mirror_send(0, 3)
+    hop(1, 0)
     mirror_send(5, 0)
+    mirror_send(3, 0)
+    mirror_send(6, 0)
+    mirror_send(4, 2)
+    mirror_send(2, 2)
+    swapped()
+    mirror_send(5, 2)
+    squares()
+    mirror_send(1, 1)
+    hop(0, 1)
+    x_first(1, 0)
+    mirror_send(7, 3)
+    mirror_send(6, 3)
+    mirror_send(2, 1)
+    mirror_send(6, 2)
+    mirror_send(2, 0)
+    mirror_send(0, 1)
+    mirror_send(2, 3)
+    mirror_send(1, 3)
+    mirror_send(6, 1)
+    hop(1, 1)
+    mirror_send(4, 1)
+    mirror_send(7, 1)
+    mirror_send(1, 0)
+    mirror_send(0, 2)
+    hop(0, 2)
     mirror_send(7, 2)
-    mirror_send(2, 0)
-    mirror_send(2, 3)
-    mirror_send(0, 1)
-    mirror_send(6, 3)
-    mirror_send(1, 0)
-    swapped()
-    mirror_send(7, 3)
-    hop(0, 0)
+    mirror_regroup(2)
+    mirror_send(1, 2)
+    mirror_send(3, 2)
+    mirror_send(3, 3)
     mirror_send(5, 1)
-    mirror_send(2, 2)
-    mirror_send(3, 1)
-    mirror_send(1, 1)
-    mirror_send(3, 0)
-    mirror_send(0, 2)
-    mirror_send(6, 1)
-    mirror_send(0, 3)
-    x_first(1, 0)
-    hop(1, 0)
-    mirror_send(5, 2)
-    hop(0, 1)
-    mirror_send(7, 1)
-    mirror_send(3, 2)
-    mirror_send(1, 2)
-    mirror_send(3, 3)
     x_first(1, 1)
     mirror_regroup(0)
+    mirror_send(7, 0)
+    mirror_send(5, 3)
+    mirror_send(4, 3)
     forward(0, 0)
-    mirror_send(6, 0)
-    mirror_send(1, 3)
-    squares()
-    mirror_send(5, 3)
-    mirror_send(4, 1)
-    mirror_send(6, 2)
+    mirror_send(3, 1)
+    hop(0, 3)
     forward(0, 1)
-    mirror_send(7, 0)
-    hop(0, 2)
-    hop(1, 1)
-    mirror_send(2, 1)
-    mirror_send(4, 2)
-    mirror_regroup(5)
-    mirror_send(4, 3)
-    forward(1, 0)
-    mirror_regroup(3)
+    forward(1, 1)
+    mirror_regroup(6)
     x_first(1, 2)
     forward(0, 2)
-    mirror_regroup(6)
     mirror_regroup(1)
-    sigma(5)
-    hop(0, 3)
+    mirror_regroup(7)
+    forward(0, 3)
+    mirror_regroup(5)
     mirror_send(4, 0)
     hop(1, 2)
-    mirror_regroup(7)
-    sigma(6)
-    mirror_regroup(2)
-    forward(0, 3)
+    mirror_regroup(3)
+    sigma(7)
+    hop(0, 4)
     x_first(1, 3)
-    sigma(1)
-    hop(0, 4)
+    sigma(0)
+    sigma(2)
+    forward(1, 0)
     mirror_regroup(4)
     hop(1, 3)
-    sigma(0)
+    sigma(6)
+    sigma(5)
     x_first(1, 4)
+    sigma(1)
     forward(0, 4)
     sigma(3)
-    sigma(2)
+    last(0, 0)
     hop(1, 4)
-    forward(1, 1)
     sigma(4)
-    sigma(7)
+    forward(1, 2)
+    sigmas_landed(0)
     forward(1, 3)
+    last(0, 1)
     x_first(1, 5)
-    last(0, 1)
-    forward(1, 2)
-    last(0, 0)
     forward(1, 4)
     sigmas_landed(1)
-    sigmas_landed(0)
     multiply(0)
     last(1, 0)
     x_first(1, 6)
@@ -476,6 +501,7 @@
             pltpu.SMEM((64,), jnp.int32),
             pltpu.VMEM((16, 128), F32),
             pltpu.VMEM((2, 2, 64, 16, 128), BF),
+            pltpu.VMEM((2, 8, 16, 128), BF),
             pltpu.VMEM((NR, 2, 2, 2, 16, 128), BF),
             pltpu.VMEM((NR, 2, 2, 2, 16, 128), BF),
             pltpu.VMEM((NZ, NMODE, 2, 2, 16, 128), BF),
@@ -487,10 +513,10 @@
             pltpu.VMEM((4, 4, NY, NCORE, 16, 128), BF),
             pltpu.VMEM((2, NY, 4, 4, 16, 128), BF),
             pltpu.VMEM((2, 9, 8, 128), F32),
-            dma((4,)), dma((8,)), dma((1,)), dma((NR,)), dma((1,)), dma((NZ, NMODE)),
+            dma((4,)), dma((16,)), dma((1,)), dma((NR,)), dma((1,)), dma((NZ, NMODE)),
             dma((len(CHUNK), 2, 4)), dma((len(CHUNK), 2, 4)), dma((len(CHUNK), NZ, 4)), dma((len(CHUNK), NZ, 4)),
             dma((len(CHUNK), 4)), dma((len(CHUNK), 4)), dma((len(CHUNK), 2, 4)), dma((len(CHUNK), 2, 4)),
-            dma((8,)), dma((8,)), dma((NZ,)), dma((NZ,)), dma((len(PIECE), 2, NY)), dma((len(PIECE), 2, NY)),
+            dma((len(CHUNK), 3, 2)), dma((1,)), dma((1,)), dma((NZ,)), dma((NZ,)), dma((len(PIECE), 2, NY)), dma((len(PIECE), 2, NY)),
         ],
         compiler_params=pltpu.CompilerParams(
             collective_id=0, has_side_effects=True, vmem_limit_bytes=40 * 1024 * 1024

time: 68.4 us -> 68 us (level)
  no operation moved by 1% of the time
where the time goes in v6:
time: 68 us; the launch traced here: 67.9 us
  Pallas kernels  67.2 us (99%)
  local copies, waits for them, and re-layouts  0.71 us (1%)
    pallas_call x1, Pallas kernels, body(): pl.pallas_call(kernel, out_shape=jax.ShapeDtypeStruct((2, 2, 8, 16, 128),...  67.2 us

profile of v6, /device:TPU:1, one launch (start us, length us, event | category | flops | bytes accessed | tf_op | source)
XLA Modules:
  0.0 67.9 jit_solution(10213025518999034768)
XLA Ops:
  0.0 67.2 %shard_map.55 = f32[2,2,8,16,128]{4,3,2,1,0:T(8,128)S(1)} custom-call(s32[64]{0:T(128)} %rt_hbm.1, s32[64]{0:T(128)} %ds_hbm.1, f32[16,128]{1,0:T(8,128)} %dl_hbm.1, bf16[2,2,64,16,128]{4,3,2,1,0:T(8,128)(2,1)} %g_hbm.1, bf16[2,2,8,16,128]{4,3,2,1,0:T(8,128)(2,1)} %c_hbm.1), custom_call_target="tpu_custom_call" | custom-call | flops 2147483648 | bytes 1600000 | tf_op jit(solution)/shard_map/pallas_call | solution.py:494
  67.2 0.7 %copy.7 = f32[2,2,8,16,128]{4,3,2,1,0:T(8,128)} copy(f32[2,2,8,16,128]{4,3,2,1,0:T(8,128)S(1)} %shard_map.55) | data formatting | bytes 524288
